TPU v7x, 128 devices: a whole 4x4x4 slice. The times are simulated.
128 devices in a mesh: leaf: 4 (over z), dev: 32 (over y, x, core).
Axes of the slice: x: 4, y: 4, z: 4, core: 2. Of those that a mesh axis runs over, the one named last changes fastest.
Arguments:
- panel_coords: float32 [3, 2097152], P(None, ('leaf', 'dev')), may hold values from -2 to 2
- panel_weights: float32 [2097152], P(('leaf', 'dev')), may hold values from 0.25 to 4
- panel_order: int32 [128, 16384], P(('leaf', 'dev')), may hold values from 0 to 16383, each once within a row
- row_owner: int32 [4096, 1], P(('leaf', 'dev')), may hold values from 0 to 31; in each aligned block of 32 rows (0 to 31, 32 to 63, ...) at most 2 rows name the same one
- col_owner: int32 [4096, 1], P(('leaf', 'dev')), may hold values from 0 to 31; in each aligned block of 32 rows (0 to 31, 32 to 63, ...) at most 2 rows name the same one
- pair_slots: int32 [4096, 2], P(('leaf', 'dev')), may hold values from 0 to 15
- rank_blocks: int32 [4096], P(('leaf', 'dev')), may hold values from 1 to 4
- sketch: bfloat16 [4096, 1024, 128], P(('leaf', 'dev')), may hold values from -0.1875 to 0.1875
Outputs:
- range_sketch: bfloat16 [4096, 1024, 128], P(('leaf', 'dev'))
- co_sketch: bfloat16 [4096, 128, 1024], P(('leaf', 'dev'))
Inputs may be any that keep to these rules, and one draw needn't show every extreme that they name: `row_owner`: in the rows of one device, each value is named by at most 2 rows; the value is a member index inside the device's own subtree group. `col_owner`: in the rows of one device, each value is named by at most 2 rows; the value is a member index inside the device's own subtree group. `panel_order`: each row is a permutation.
All inputs are finite; a program needn't handle non-finite values.
Results may differ from a plain program's by a relative error of at most 0.005.
Values sent between devices are 32-bit elements; how exact they have to be, the bound alone decides.
No kernel may reach another device: no remote copies, remote signals or barrier semaphores. Data moves between devices by JAX's collectives and lax.ppermute only.
A program may use at most 192 MiB of HBM per device.

v0:
```python
import math

import jax
import jax.numpy as jnp
from jax import lax
from jax.sharding import PartitionSpec as P

PTS = 1024
BLK = 32
CL_DEV = 16


softening = 0.01
group_size = 4


def interaction(row_points, col_points):
    delta_x = row_points[:, 0, :, None] - col_points[:, 0, None, :]
    delta_y = row_points[:, 1, :, None] - col_points[:, 1, None, :]
    delta_z = row_points[:, 2, :, None] - col_points[:, 2, None, :]
    squared = delta_x * delta_x + delta_y * delta_y + delta_z * delta_z + softening
    return (col_points[:, 3, None, :] / jnp.sqrt(squared)).astype(jnp.bfloat16)


def both_products(kernel, operand, scale):
    ranged = jnp.einsum("gij,gjr->gir", kernel, operand, preferred_element_type=jnp.float32).astype(
        jnp.bfloat16
    )
    product = jnp.einsum("gir,gij->grj", ranged, kernel, preferred_element_type=jnp.float32)
    return (ranged, (product * scale).astype(jnp.bfloat16))


def padded_group(operands):
    row_points, col_points, test_matrix, rank = operands
    kernel = interaction(row_points, col_points)
    scale = 1.0 / math.sqrt(kernel.shape[1])
    active = (
        lax.broadcasted_iota(jnp.int32, (rank.shape[0], 1, test_matrix.shape[2]), 2)
        < (rank * BLK)[:, None, None]
    )
    masked = jnp.where(active, test_matrix, jnp.zeros_like(test_matrix))
    return both_products(kernel, masked, scale)


def grouped(array):
    return array.reshape((array.shape[0] // group_size, group_size) + array.shape[1:])


def shards(
    panel_coords, panel_weights, panel_order, row_owner, col_owner, pair_slots, rank_blocks, sketch
):
    order = panel_order[0]
    stacked = jnp.concatenate([panel_coords, panel_weights[None, :]], axis=0)
    picked = jnp.take(stacked, order, axis=1)
    local_points = picked.reshape(4, CL_DEV, PTS).transpose(1, 0, 2)
    count = rank_blocks.shape[0]
    members = lax.axis_size("dev")
    capacity = max(2, 2 * count // members)
    owners = jnp.stack([row_owner[:, 0], col_owner[:, 0]], axis=0)
    onehot = (owners[:, :, None] == jnp.arange(members, dtype=jnp.int32)[None, None, :]).astype(
        jnp.int32
    )
    earlier = jnp.cumsum(onehot, axis=1) - onehot
    position = jnp.sum(earlier * onehot, axis=2)
    side = jnp.broadcast_to(jnp.arange(2, dtype=jnp.int32)[:, None], owners.shape)
    wanted = jnp.zeros((members, 2, capacity), jnp.int32)
    wanted = wanted.at[owners, side, position].set(pair_slots.T)
    found = local_points[lax.all_to_all(wanted, "dev", split_axis=0, concat_axis=0, tiled=True)]
    replies = lax.all_to_all(found, "dev", split_axis=0, concat_axis=0, tiled=True)
    row_points = replies[owners[0], 0, position[0]]
    col_points = replies[owners[1], 1, position[1]]
    operands = (grouped(row_points), grouped(col_points), grouped(sketch), grouped(rank_blocks))
    range_sketch, co_sketch = lax.map(padded_group, operands)
    range_sketch = range_sketch.reshape((count,) + range_sketch.shape[2:])
    co_sketch = co_sketch.reshape((count,) + co_sketch.shape[2:])
    return (range_sketch, co_sketch)


def solution(mesh):
    in_specs = (
        P(None, ("leaf", "dev")),
        P(("leaf", "dev")),
        P(("leaf", "dev"), None),
        P(("leaf", "dev"), None),
        P(("leaf", "dev"), None),
        P(("leaf", "dev"), None),
        P(("leaf", "dev")),
        P(("leaf", "dev"), None, None),
    )
    out_specs = (P(("leaf", "dev"), None, None), P(("leaf", "dev"), None, None))
    return jax.shard_map(shards, mesh=mesh, in_specs=in_specs, out_specs=out_specs, check_vma=False)
```

profile of v0, /device:TPU:1, one launch (start us, length us, event | category | flops | bytes accessed | tf_op | source)
XLA Modules:
  0.0 334.8 jit_solution(8636297831898030820)
XLA Ops:
  0.6 0.7 pad_add_fusion
  1.3 0.1 fusion.14
  1.4 0.1 reduce_window_sum.11
  1.4 0.2 select_reduce_fusion
  1.6 0.7 fusion.18
  2.3 0.1 reshape.293
  2.4 0.8 reshape.295
  3.2 0.0 copy-start.1
  3.2 0.0 copy-start
  3.2 0.0 copy-start.2
  3.2 4.4 %scatter_fusion = s32[32,2,2]{0,2,1:T(2,128)S(1)} fusion(s32[32,2,2]{0,2,1:T(2,128)S(1)} %broadcast.159, s32[64]{0:T(128)S(1)} %reshape.293, s32[64]{0:T(128)S(1)} %reshape.295), kind=kCustom, calls=%fused_computation.4 | custom fusion | bytes 1536 | tf_op jit(solution)/shard_map/scatter | solution.py:67
  7.6 0.7 copy.40
  8.3 8.6 %all-to-all-start = ((s32[32,2,2]{2,1,0:T(2,128)}), s32[32,2,2]{2,1,0:T(2,128)S(1)}, u32[]{:S(2)}, u32[]{:S(2)}) async-start(s32[32,2,2]{2,1,0:T(2,128)} %copy.40), calls=%async_computation | async-start | bytes 65536 | tf_op jit(solution)/shard_map/all_to_all | solution.py:68
  16.9 0.0 copy-done.1
  16.9 0.1 compare_select_fusion
  17.0 0.5 broadcast.292
  17.5 0.8 reduce.7
  18.4 0.0 copy-done
  18.4 0.0 copy-done.2
  18.4 0.1 pad_maximum_fusion
  18.5 5.1 %copy.36 = f32[4,16384]{0,1:T(8,128)} copy(f32[4,16384]{1,0:T(4,128)S(1)} %pad_maximum_fusion) | data formatting | bytes 524288 | tf_op jit(solution)/shard_map/concatenate | solution.py:53
  23.6 58.2 %gather_fusion = f32[16384,4]{1,0:T(8,128)} fusion(f32[4,16384]{0,1:T(8,128)} %copy.36, s32[16384]{0:T(1024)S(1)} %broadcast_clamp_fusion), kind=kCustom, calls=%fused_computation | custom fusion | bytes 589824 | tf_op jit(solution)/shard_map/jit(_take)/gather | solution.py:54
  81.8 9.9 %select_bitcast_fusion = f32[16,4,1024]{1,2,0:T(8,128)} fusion(f32[4,16,1024]{0,2,1:T(8,128)} %bitcast.89, pred[16,1024]{1,0:T(8,128)(4,1)S(1)} %compare_and_fusion), kind=kLoop, calls=%fused_computation.36 | loop fusion | flops 65536 | bytes 540672 | tf_op jit(solution)/shard_map/transpose | solution.py:55
  91.7 0.0 all-to-all-done
  91.7 0.1 copy.41
  91.8 0.1 copy.44
  91.9 0.2 reshape.275
  92.1 26.7 %gather_fusion.1 = f32[128,4,1024]{1,2,0:T(8,128)} fusion(f32[16,4,1024]{1,2,0:T(8,128)} %select_bitcast_fusion, s32[1024]{0:T(1024)S(1)} %pad_clamp_fusion), kind=kCustom, calls=%fused_computation.1 | custom fusion | bytes 4194816 | tf_op jit(solution)/shard_map/gather | solution.py:68
  118.8 0.0 copy-start.5
  118.8 0.0 copy-start.4
  118.8 35.2 %copy.45 = f32[128,4,1024]{2,1,0:T(4,128)} copy(f32[128,4,1024]{1,2,0:T(8,128)} %gather_fusion.1) | data formatting | bytes 4194304 | tf_op jit(solution)/shard_map/gather | solution.py:68
  154.1 7.5 %all-to-all-start.1 = ((f32[32,2,2,4,1024]{4,3,2,1,0:T(4,128)}), f32[32,2,2,4,1024]{4,3,2,1,0:T(4,128)S(1)}, u32[]{:S(2)}, u32[]{:S(2)}) async-start(f32[32,2,2,4,1024]{4,3,2,1,0:T(4,128)} %bitcast.28), calls=%async_computation.1 | async-start | bytes 4194304 | tf_op jit(solution)/shard_map/all_to_all | solution.py:69
  161.6 0.0 copy-done.5
  161.6 0.1 reshape.261
  161.6 0.0 copy-done.3
  161.7 0.0 copy-done.4
  161.7 27.7 %all-to-all-done.1 = f32[32,2,2,4,1024]{4,3,2,1,0:T(4,128)S(1)} async-done(((f32[32,2,2,4,1024]{4,3,2,1,0:T(4,128)}), f32[32,2,2,4,1024]{4,3,2,1,0:T(4,128)S(1)}, u32[]{:S(2)}, u32[]{:S(2)}) %all-to-all-start.1) | async-done | bytes 2097184 | tf_op jit(solution)/shard_map/all_to_all | solution.py:69
  189.4 0.9 gather_fusion.2
  190.3 0.9 gather_fusion.3
  191.2 143.6 %while.12 = (s32[]{:T(128)}, bf16[8,4,1024,128]{3,2,1,0:T(8,128)(2,1)}, bf16[8,4,128,1024]{3,2,1,0:T(8,128)(2,1)}, f32[8,4,4,1024]{3,2,1,0:T(4,128)S(1)}, f32[8,...) while((s32[]{:T(128)}, ...), condition=%wide.region_4.5_spmd, body=%wide.region_3.4_spmd.sunk | while | flops 2241856000 | bytes 6228621 | solution.py:73
  191.4 0.1 iota_compare_fusion.3
  191.4 9.0 %bitcast_dynamic-update-slice_fusion.2 = (bf16[8,4,1024,128]{3,2,1,0:T(8,128)(2,1)}, bf16[4,1024,128]{2,1,0:T(8,128)(2,1)S(1)}) fusion(bf16[8,4,1024,128]{3,2,1,0:T(8,128)(2,1)} %get-tuple-element.164, s32[]{:T(128)} %get-tuple-element.163, bf16[8,4,1024,128]{3,2,1,0:T(8,128)(2,1)} %get-tuple-element.177, ...), kind=kOutput, calls=%fused_computation.12.clone.1 | convolution fusion | flops 1120927744 | bytes 3261952 | tf_op jit(solution)/shard_map/while/body/eval_jaxpr/gij,gjr->gir/dot_general | solution.py:26
  200.5 8.7 %fusion.38 = bf16[8,4,128,1024]{3,2,1,0:T(8,128)(2,1)} fusion(bf16[8,4,128,1024]{3,2,1,0:T(8,128)(2,1)} %get-tuple-element.165, s32[]{:T(128)} %get-tuple-element.163, bf16[4,1024,128]{2,1,0:T(8,128)(2,1)S(1)} %get-tuple-element.154, f32[4,1024]{1,0:T(4,128)S(1)} %get-tuple-element.145, f32[4,1024]{1,0:T(4,128)S(1)} %get-tuple-element.147, ...), kind=kOutput, calls=%fused_computation.11.clone.1 | convolution fusion | flops 1120927744 | bytes 2212352 | tf_op jit(solution)/shard_map/while/body/eval_jaxpr/gir,gij->grj/dot_general | solution.py:29
  209.3 0.1 iota_compare_fusion.3
  209.4 9.0 %bitcast_dynamic-update-slice_fusion.2 = (bf16[8,4,1024,128]{3,2,1,0:T(8,128)(2,1)}, bf16[4,1024,128]{2,1,0:T(8,128)(2,1)S(1)}) fusion(bf16[8,4,1024,128]{3,2,1,0:T(8,128)(2,1)} %get-tuple-element.164, s32[]{:T(128)} %get-tuple-element.163, bf16[8,4,1024,128]{3,2,1,0:T(8,128)(2,1)} %get-tuple-element.177, ...), kind=kOutput, calls=%fused_computation.12.clone.1 | convolution fusion | flops 1120927744 | bytes 3261952 | tf_op jit(solution)/shard_map/while/body/eval_jaxpr/gij,gjr->gir/dot_general | solution.py:26
  218.4 8.7 %fusion.38 = bf16[8,4,128,1024]{3,2,1,0:T(8,128)(2,1)} fusion(bf16[8,4,128,1024]{3,2,1,0:T(8,128)(2,1)} %get-tuple-element.165, s32[]{:T(128)} %get-tuple-element.163, bf16[4,1024,128]{2,1,0:T(8,128)(2,1)S(1)} %get-tuple-element.154, f32[4,1024]{1,0:T(4,128)S(1)} %get-tuple-element.145, f32[4,1024]{1,0:T(4,128)S(1)} %get-tuple-element.147, ...), kind=kOutput, calls=%fused_computation.11.clone.1 | convolution fusion | flops 1120927744 | bytes 2212352 | tf_op jit(solution)/shard_map/while/body/eval_jaxpr/gir,gij->grj/dot_general | solution.py:29
  227.2 0.1 iota_compare_fusion.3
  227.3 9.0 %bitcast_dynamic-update-slice_fusion.2 = (bf16[8,4,1024,128]{3,2,1,0:T(8,128)(2,1)}, bf16[4,1024,128]{2,1,0:T(8,128)(2,1)S(1)}) fusion(bf16[8,4,1024,128]{3,2,1,0:T(8,128)(2,1)} %get-tuple-element.164, s32[]{:T(128)} %get-tuple-element.163, bf16[8,4,1024,128]{3,2,1,0:T(8,128)(2,1)} %get-tuple-element.177, ...), kind=kOutput, calls=%fused_computation.12.clone.1 | convolution fusion | flops 1120927744 | bytes 3261952 | tf_op jit(solution)/shard_map/while/body/eval_jaxpr/gij,gjr->gir/dot_general | solution.py:26
  236.3 8.7 %fusion.38 = bf16[8,4,128,1024]{3,2,1,0:T(8,128)(2,1)} fusion(bf16[8,4,128,1024]{3,2,1,0:T(8,128)(2,1)} %get-tuple-element.165, s32[]{:T(128)} %get-tuple-element.163, bf16[4,1024,128]{2,1,0:T(8,128)(2,1)S(1)} %get-tuple-element.154, f32[4,1024]{1,0:T(4,128)S(1)} %get-tuple-element.145, f32[4,1024]{1,0:T(4,128)S(1)} %get-tuple-element.147, ...), kind=kOutput, calls=%fused_computation.11.clone.1 | convolution fusion | flops 1120927744 | bytes 2212352 | tf_op jit(solution)/shard_map/while/body/eval_jaxpr/gir,gij->grj/dot_general | solution.py:29
  245.2 0.1 iota_compare_fusion.3
  245.3 9.0 %bitcast_dynamic-update-slice_fusion.2 = (bf16[8,4,1024,128]{3,2,1,0:T(8,128)(2,1)}, bf16[4,1024,128]{2,1,0:T(8,128)(2,1)S(1)}) fusion(bf16[8,4,1024,128]{3,2,1,0:T(8,128)(2,1)} %get-tuple-element.164, s32[]{:T(128)} %get-tuple-element.163, bf16[8,4,1024,128]{3,2,1,0:T(8,128)(2,1)} %get-tuple-element.177, ...), kind=kOutput, calls=%fused_computation.12.clone.1 | convolution fusion | flops 1120927744 | bytes 3261952 | tf_op jit(solution)/shard_map/while/body/eval_jaxpr/gij,gjr->gir/dot_general | solution.py:26
  254.3 8.7 %fusion.38 = bf16[8,4,128,1024]{3,2,1,0:T(8,128)(2,1)} fusion(bf16[8,4,128,1024]{3,2,1,0:T(8,128)(2,1)} %get-tuple-element.165, s32[]{:T(128)} %get-tuple-element.163, bf16[4,1024,128]{2,1,0:T(8,128)(2,1)S(1)} %get-tuple-element.154, f32[4,1024]{1,0:T(4,128)S(1)} %get-tuple-element.145, f32[4,1024]{1,0:T(4,128)S(1)} %get-tuple-element.147, ...), kind=kOutput, calls=%fused_computation.11.clone.1 | convolution fusion | flops 1120927744 | bytes 2212352 | tf_op jit(solution)/shard_map/while/body/eval_jaxpr/gir,gij->grj/dot_general | solution.py:29
  263.1 0.1 iota_compare_fusion.3
  263.2 9.0 %bitcast_dynamic-update-slice_fusion.2 = (bf16[8,4,1024,128]{3,2,1,0:T(8,128)(2,1)}, bf16[4,1024,128]{2,1,0:T(8,128)(2,1)S(1)}) fusion(bf16[8,4,1024,128]{3,2,1,0:T(8,128)(2,1)} %get-tuple-element.164, s32[]{:T(128)} %get-tuple-element.163, bf16[8,4,1024,128]{3,2,1,0:T(8,128)(2,1)} %get-tuple-element.177, ...), kind=kOutput, calls=%fused_computation.12.clone.1 | convolution fusion | flops 1120927744 | bytes 3261952 | tf_op jit(solution)/shard_map/while/body/eval_jaxpr/gij,gjr->gir/dot_general | solution.py:26
  272.2 8.7 %fusion.38 = bf16[8,4,128,1024]{3,2,1,0:T(8,128)(2,1)} fusion(bf16[8,4,128,1024]{3,2,1,0:T(8,128)(2,1)} %get-tuple-element.165, s32[]{:T(128)} %get-tuple-element.163, bf16[4,1024,128]{2,1,0:T(8,128)(2,1)S(1)} %get-tuple-element.154, f32[4,1024]{1,0:T(4,128)S(1)} %get-tuple-element.145, f32[4,1024]{1,0:T(4,128)S(1)} %get-tuple-element.147, ...), kind=kOutput, calls=%fused_computation.11.clone.1 | convolution fusion | flops 1120927744 | bytes 2212352 | tf_op jit(solution)/shard_map/while/body/eval_jaxpr/gir,gij->grj/dot_general | solution.py:29
  281.1 0.1 iota_compare_fusion.3
  281.2 9.0 %bitcast_dynamic-update-slice_fusion.2 = (bf16[8,4,1024,128]{3,2,1,0:T(8,128)(2,1)}, bf16[4,1024,128]{2,1,0:T(8,128)(2,1)S(1)}) fusion(bf16[8,4,1024,128]{3,2,1,0:T(8,128)(2,1)} %get-tuple-element.164, s32[]{:T(128)} %get-tuple-element.163, bf16[8,4,1024,128]{3,2,1,0:T(8,128)(2,1)} %get-tuple-element.177, ...), kind=kOutput, calls=%fused_computation.12.clone.1 | convolution fusion | flops 1120927744 | bytes 3261952 | tf_op jit(solution)/shard_map/while/body/eval_jaxpr/gij,gjr->gir/dot_general | solution.py:26
  290.2 8.7 %fusion.38 = bf16[8,4,128,1024]{3,2,1,0:T(8,128)(2,1)} fusion(bf16[8,4,128,1024]{3,2,1,0:T(8,128)(2,1)} %get-tuple-element.165, s32[]{:T(128)} %get-tuple-element.163, bf16[4,1024,128]{2,1,0:T(8,128)(2,1)S(1)} %get-tuple-element.154, f32[4,1024]{1,0:T(4,128)S(1)} %get-tuple-element.145, f32[4,1024]{1,0:T(4,128)S(1)} %get-tuple-element.147, ...), kind=kOutput, calls=%fused_computation.11.clone.1 | convolution fusion | flops 1120927744 | bytes 2212352 | tf_op jit(solution)/shard_map/while/body/eval_jaxpr/gir,gij->grj/dot_general | solution.py:29
  299.0 0.1 iota_compare_fusion.3
  299.1 9.0 %bitcast_dynamic-update-slice_fusion.2 = (bf16[8,4,1024,128]{3,2,1,0:T(8,128)(2,1)}, bf16[4,1024,128]{2,1,0:T(8,128)(2,1)S(1)}) fusion(bf16[8,4,1024,128]{3,2,1,0:T(8,128)(2,1)} %get-tuple-element.164, s32[]{:T(128)} %get-tuple-element.163, bf16[8,4,1024,128]{3,2,1,0:T(8,128)(2,1)} %get-tuple-element.177, ...), kind=kOutput, calls=%fused_computation.12.clone.1 | convolution fusion | flops 1120927744 | bytes 3261952 | tf_op jit(solution)/shard_map/while/body/eval_jaxpr/gij,gjr->gir/dot_general | solution.py:26
  308.1 8.7 %fusion.38 = bf16[8,4,128,1024]{3,2,1,0:T(8,128)(2,1)} fusion(bf16[8,4,128,1024]{3,2,1,0:T(8,128)(2,1)} %get-tuple-element.165, s32[]{:T(128)} %get-tuple-element.163, bf16[4,1024,128]{2,1,0:T(8,128)(2,1)S(1)} %get-tuple-element.154, f32[4,1024]{1,0:T(4,128)S(1)} %get-tuple-element.145, f32[4,1024]{1,0:T(4,128)S(1)} %get-tuple-element.147, ...), kind=kOutput, calls=%fused_computation.11.clone.1 | convolution fusion | flops 1120927744 | bytes 2212352 | tf_op jit(solution)/shard_map/while/body/eval_jaxpr/gir,gij->grj/dot_general | solution.py:29
  317.0 0.1 iota_compare_fusion.3
  317.0 9.0 %bitcast_dynamic-update-slice_fusion.2 = (bf16[8,4,1024,128]{3,2,1,0:T(8,128)(2,1)}, bf16[4,1024,128]{2,1,0:T(8,128)(2,1)S(1)}) fusion(bf16[8,4,1024,128]{3,2,1,0:T(8,128)(2,1)} %get-tuple-element.164, s32[]{:T(128)} %get-tuple-element.163, bf16[8,4,1024,128]{3,2,1,0:T(8,128)(2,1)} %get-tuple-element.177, ...), kind=kOutput, calls=%fused_computation.12.clone.1 | convolution fusion | flops 1120927744 | bytes 3261952 | tf_op jit(solution)/shard_map/while/body/eval_jaxpr/gij,gjr->gir/dot_general | solution.py:26
  326.1 8.7 %fusion.38 = bf16[8,4,128,1024]{3,2,1,0:T(8,128)(2,1)} fusion(bf16[8,4,128,1024]{3,2,1,0:T(8,128)(2,1)} %get-tuple-element.165, s32[]{:T(128)} %get-tuple-element.163, bf16[4,1024,128]{2,1,0:T(8,128)(2,1)S(1)} %get-tuple-element.154, f32[4,1024]{1,0:T(4,128)S(1)} %get-tuple-element.145, f32[4,1024]{1,0:T(4,128)S(1)} %get-tuple-element.147, ...), kind=kOutput, calls=%fused_computation.11.clone.1 | convolution fusion | flops 1120927744 | bytes 2212352 | tf_op jit(solution)/shard_map/while/body/eval_jaxpr/gir,gij->grj/dot_general | solution.py:29
  (58 shorter events, 1.1 us)
Async XLA Ops:
  3.2 13.7 %copy-start.1 = (s32[1,16384]{1,0:T(1,128)S(1)}, s32[1,16384]{1,0:T(1,128)}, u32[]{:S(2)}) copy-start(s32[1,16384]{1,0:T(1,128)} %param.12) | copy-start | bytes 196612
  3.2 15.2 %copy-start = (f32[3,16384]{1,0:T(4,128)S(1)}, f32[3,16384]{1,0:T(4,128)}, u32[]{:S(2)}) copy-start(f32[3,16384]{1,0:T(4,128)} %param.10) | copy-start | bytes 589828
  3.2 15.2 %copy-start.2 = (f32[16384]{0:T(1024)S(1)}, f32[16384]{0:T(1024)}, u32[]{:S(2)}) copy-start(f32[16384]{0:T(1024)} %param.11) | copy-start | bytes 196612
  8.3 83.4 %all-to-all-start = ((s32[32,2,2]{2,1,0:T(2,128)}), s32[32,2,2]{2,1,0:T(2,128)S(1)}, u32[]{:S(2)}, u32[]{:S(2)}) async-start(s32[32,2,2]{2,1,0:T(2,128)} %copy.40), calls=%async_computation | async-start | bytes 65536 | tf_op jit(solution)/shard_map/all_to_all | solution.py:68
  118.8 42.7 %copy-start.5 = (s32[32]{0:T(128)S(1)}, s32[32]{0:T(128)}, u32[]{:S(2)}) copy-start(s32[32]{0:T(128)} %param.16) | copy-start | bytes 388
  118.8 42.8 %copy-start.3 = (s32[32,1]{0,1:T(1,128)S(1)}, s32[32,1]{0,1:T(1,128)}, u32[]{:S(2)}) copy-start(s32[32,1]{0,1:T(1,128)} %param.14) | copy-start | bytes 388
  118.8 42.8 %copy-start.4 = (s32[32,1]{0,1:T(1,128)S(1)}, s32[32,1]{0,1:T(1,128)}, u32[]{:S(2)}) copy-start(s32[32,1]{0,1:T(1,128)} %param.13) | copy-start | bytes 388
  154.1 35.3 %all-to-all-start.1 = ((f32[32,2,2,4,1024]{4,3,2,1,0:T(4,128)}), f32[32,2,2,4,1024]{4,3,2,1,0:T(4,128)S(1)}, u32[]{:S(2)}, u32[]{:S(2)}) async-start(f32[32,2,2,4,1024]{4,3,2,1,0:T(4,128)} %bitcast.28), calls=%async_computation.1 | async-start | bytes 4194304 | tf_op jit(solution)/shard_map/all_to_all | solution.py:69
where the time goes:
time: 337 us; the launch traced here: 335 us
  matrix products  142 us (42%)
  local copies, waits for them, and re-layouts  135 us (40%)
  waiting for transfers between devices  27.7 us (8%)
  starting transfers between devices  16 us (5%)
  other arithmetic  13.4 us (4%)
    dot_general x8, matrix products, both_products(): jnp.einsum('gij,gjr->gir', kernel, operand, preferred_element_type=jnp.fl...  72.2 us
    dot_general x8, matrix products, both_products(): jnp.einsum('gir,gij->grj', ranged, kernel, preferred_element_type=jnp.flo...  69.4 us
    gather x2, local copies, waits for them, and re-layouts, shards(): local_points[lax.all_to_all(wanted, 'dev', split_axis=0, concat_axis=0, t...  62 us
    gather x1, local copies, waits for them, and re-layouts, shards(): picked = jnp.take(stacked, order, axis=1)  58.2 us
    all_to_all x1, waiting for transfers between devices, shards(): lax.all_to_all(found, 'dev', split_axis=0, concat_axis=0, tiled=True)  27.7 us
    transpose x1, other arithmetic, shards(): local_points = picked.reshape(4, CL_DEV, PTS).transpose(1, 0, 2)  9.91 us
    all_to_all x1, starting transfers between devices, shards(): lax.all_to_all(wanted, 'dev', split_axis=0, concat_axis=0, tiled=True)  8.59 us
    all_to_all x1, starting transfers between devices, shards(): lax.all_to_all(found, 'dev', split_axis=0, concat_axis=0, tiled=True)  7.46 us
  transfers between devices with their start and end apart: 2, of which 1 were waited for; matrix products, arithmetic and copies ran while one was open for 22% of the time, Pallas kernels for 0%

commit v1 on v0

v1 whole, which is shorter than its diff:
```python
import functools
import math

import jax
import jax.numpy as jnp
from jax import lax
from jax.experimental import pallas as pl
from jax.experimental.pallas import tpu as pltpu
from jax.sharding import PartitionSpec as P

PTS = 1024
RK = 128
BLK = 32
CL_DEV = 16
CHUNK = 256

softening = 0.01
bf16 = jnp.bfloat16
f32 = jnp.float32


def contract(a, b, dim_a, dim_b):
    return lax.dot_general(a, b, (((dim_a,), (dim_b,)), ((), ())), preferred_element_type=f32)


def pick_kernel(order_ref, coords_ref, weights_ref, out_ref):
    unroll = 32
    for cluster in range(CL_DEV):
        index = order_ref[cluster * 8 : cluster * 8 + 8, :]
        high = index >> 7
        low = index & 127

        def step(turn, picked):
            picked = list(picked)
            for inner in range(unroll):
                row = turn * unroll + inner
                here = high == row
                for part in range(4):
                    if part < 3:
                        line = coords_ref[part, pl.ds(row, 1), :]
                    else:
                        line = weights_ref[pl.ds(row, 1), :]
                    line = jnp.broadcast_to(line, (8, 128))
                    found = jnp.take_along_axis(line, low, axis=1, mode="promise_in_bounds")
                    picked[part] = jnp.where(here, found, picked[part])
            return tuple(picked)

        zero = jnp.zeros((8, 128), f32)
        picked = lax.fori_loop(0, 128 // unroll, step, (zero,) * 4)
        for part in range(4):
            for line in range(8):
                out_ref[cluster, part : part + 1, line * 128 : line * 128 + 128] = picked[part][
                    line : line + 1, :
                ]


def pick(order, coords, weights):
    return pl.pallas_call(
        pick_kernel,
        out_shape=jax.ShapeDtypeStruct((CL_DEV, 4, PTS), f32),
        in_specs=[pl.BlockSpec(memory_space=pltpu.VMEM)] * 3,
        out_specs=pl.BlockSpec(memory_space=pltpu.VMEM),
        name="pick",
    )(order, coords, weights)


def reply_kernel(wanted_ref, points_ref, out_ref):
    first = pl.program_id(0) * out_ref.shape[0]
    for slot in range(out_ref.shape[0]):
        out_ref[slot] = points_ref[wanted_ref[first + slot]]


def reply(wanted, points):
    slots = wanted.shape[0]
    step = 16
    return pl.pallas_call(
        reply_kernel,
        grid_spec=pltpu.PrefetchScalarGridSpec(
            num_scalar_prefetch=1,
            grid=(slots // step,),
            in_specs=[pl.BlockSpec((CL_DEV, 4, PTS), lambda i, wanted: (0, 0, 0))],
            out_specs=pl.BlockSpec((step, 4, PTS), lambda i, wanted: (i, 0, 0)),
        ),
        out_shape=jax.ShapeDtypeStruct((slots, 4, PTS), f32),
        name="reply",
    )(wanted, points)


def split3(value):
    first = value.astype(bf16).astype(f32)
    rest = value - first
    second = rest.astype(bf16).astype(f32)
    return first, second, rest - second


def distance_operands(rows, cols):
    line = lax.broadcasted_iota(jnp.int32, (4, PTS), 0)
    row_square = rows[0:1] * rows[0:1] + rows[1:2] * rows[1:2] + rows[2:3] * rows[2:3]
    left = jnp.where(line < 3, rows, row_square)
    inverse = 1.0 / (cols[3:4] * cols[3:4])
    col_square = cols[0:1] * cols[0:1] + cols[1:2] * cols[1:2] + cols[2:3] * cols[2:3]
    right = jnp.where(line < 3, cols * (-2.0 * inverse), inverse)
    l1, l2, l3 = split3(left)
    r1, r2, r3 = split3(right)
    c1, c2, c3 = split3((col_square + softening) * inverse)
    ones = jnp.ones((4, PTS), f32)
    zero = jnp.zeros((4, PTS), f32)
    last = jnp.where(line == 0, c1, jnp.where(line == 1, c2, jnp.where(line == 2, c3, 0.0)))
    left = jnp.concatenate([l1, l1, l2, l1, l2, l3, ones, zero], axis=0).astype(bf16)
    right = jnp.concatenate([r1, r2, r1, r3, r2, r1, last, zero], axis=0).astype(bf16)
    return left, right


def pair_kernel(row_at, col_at, rank, rows_ref, cols_ref, sketch_ref, range_ref, co_ref):
    left, right = distance_operands(rows_ref[0], cols_ref[0])
    limit = rank[pl.program_id(0)] * BLK
    test = sketch_ref[0]
    active = lax.broadcasted_iota(jnp.int32, (1, RK), 1) < limit
    masked = jnp.where(active, test, jnp.zeros_like(test)).T

    def block(chunk):
        part = left[:, chunk * CHUNK : (chunk + 1) * CHUNK]
        return lax.rsqrt(contract(right, part, 0, 0)).astype(bf16)

    total = None
    now = block(0)
    for chunk in range(PTS // CHUNK):
        later = block(chunk + 1) if chunk + 1 < PTS // CHUNK else None
        ranged = contract(masked, now, 1, 0).astype(bf16)
        range_ref[0, chunk * CHUNK : (chunk + 1) * CHUNK, :] = ranged.T
        product = contract(ranged, now, 1, 1)
        total = product if total is None else total + product
        now = later
    co_ref[0] = (total * (1.0 / math.sqrt(PTS))).astype(bf16)


def pair_products(row_at, col_at, rank, replies, sketch):
    count = sketch.shape[0]
    return pl.pallas_call(
        pair_kernel,
        grid_spec=pltpu.PrefetchScalarGridSpec(
            num_scalar_prefetch=3,
            grid=(count,),
            in_specs=[
                pl.BlockSpec((1, 4, PTS), lambda p, row, col, rank: (row[p], 0, 0)),
                pl.BlockSpec((1, 4, PTS), lambda p, row, col, rank: (col[p], 0, 0)),
                pl.BlockSpec((1, PTS, RK), lambda p, row, col, rank: (p, 0, 0)),
            ],
            out_specs=[
                pl.BlockSpec((1, PTS, RK), lambda p, row, col, rank: (p, 0, 0)),
                pl.BlockSpec((1, RK, PTS), lambda p, row, col, rank: (p, 0, 0)),
            ],
        ),
        out_shape=[
            jax.ShapeDtypeStruct((count, PTS, RK), bf16),
            jax.ShapeDtypeStruct((count, RK, PTS), bf16),
        ],
        compiler_params=pltpu.CompilerParams(vmem_limit_bytes=48 << 20),
        name="pairs",
    )(row_at, col_at, rank, replies, replies, sketch)


def shards(
    panel_coords, panel_weights, panel_order, row_owner, col_owner, pair_slots, rank_blocks, sketch
):
    members = lax.axis_size("dev")
    me = lax.axis_index("dev")
    count = rank_blocks.shape[0]
    named = jnp.concatenate([row_owner, col_owner, pair_slots], axis=1).T
    everyone = lax.all_gather(named, "dev", axis=0, tiled=False)
    points = pick(
        panel_order.reshape(128, 128),
        panel_coords.reshape(3, 128, 128),
        panel_weights.reshape(128, 128),
    )
    mine = (everyone[:, :2, :] == me).astype(jnp.int32)
    before = jnp.cumsum(mine, axis=2) - mine
    nth = jnp.arange(2, dtype=jnp.int32)[None, None, :, None]
    chosen = mine[:, :, None, :] * (before[:, :, None, :] == nth)
    wanted = jnp.sum(chosen * everyone[:, 2:, None, :], axis=3)
    found = reply(wanted.reshape(-1), points).reshape(members, 4, 4, PTS)
    replies = lax.all_to_all(found, "dev", split_axis=0, concat_axis=0, tiled=True)
    owners = named[:2]
    same = owners[:, :, None] == owners[:, None, :]
    earlier = jnp.tril(jnp.ones((count, count), jnp.bool_), -1)
    position = jnp.sum((same & earlier[None]).astype(jnp.int32), axis=2)
    at = owners * 4 + jnp.arange(2, dtype=jnp.int32)[:, None] * 2 + position
    return tuple(
        pair_products(at[0], at[1], rank_blocks, replies.reshape(members * 4, 4, PTS), sketch)
    )


def solution(mesh):
    in_specs = (
        P(None, ("leaf", "dev")),
        P(("leaf", "dev")),
        P(("leaf", "dev"), None),
        P(("leaf", "dev"), None),
        P(("leaf", "dev"), None),
        P(("leaf", "dev"), None),
        P(("leaf", "dev")),
        P(("leaf", "dev"), None, None),
    )
    out_specs = (P(("leaf", "dev"), None, None), P(("leaf", "dev"), None, None))
    return jax.shard_map(shards, mesh=mesh, in_specs=in_specs, out_specs=out_specs, check_vma=False)
```

time: 337 us -> 147 us (0.44)
  matrix products: 142 us -> 0 us
  local copies, waits for them, and re-layouts: 135 us -> 3.19 us
  Pallas kernels: 0 us -> 81.8 us
  blocking collectives: 0 us -> 25.8 us
  other arithmetic: 13.4 us -> 1.6 us
  starting transfers between devices: 16 us -> 5.16 us
    dot_general x16 -> x0, matrix products: 142 us -> none  [the longest x8 72.2 us: both_products(): jnp.einsum('gij,gjr->gir', kernel, operand, preferred_element_type=jnp.fl...]
    gather x5 -> x0, local copies, waits for them, and re-layouts: 122 us -> none  [the longest x2 62 us: shards(): local_points[lax.all_to_all(wanted, 'dev', split_axis=0, concat_axis=0, t...]
    pallas_call x0 -> x3, Pallas kernels: none -> 81.8 us  [the longest x1 62.3 us: pair_products(): pl.pallas_call(pair_kernel, grid_spec=pltpu.PrefetchScalarGridSpec(num_sc...]
    all_gather x0 -> x1, blocking collectives: none -> 25.8 us  [shards(): everyone = lax.all_gather(named, 'dev', axis=0, tiled=False)]
    transpose x1 -> x0, other arithmetic: 9.91 us -> none  [shards(): local_points = picked.reshape(4, CL_DEV, PTS).transpose(1, 0, 2)]
    all_to_all x1 -> x0, starting transfers between devices: 8.59 us -> none  [shards(): lax.all_to_all(wanted, 'dev', split_axis=0, concat_axis=0, tiled=True)]
    concatenate x2 -> x0, local copies, waits for them, and re-layouts: 5.14 us -> none  [the longest x1 5.05 us: shards(): stacked = jnp.concatenate([panel_coords, panel_weights[None, :]], axis=0)]
    scatter x2 -> x0, local copies, waits for them, and re-layouts: 5.11 us -> none  [shards(): wanted = wanted.at[owners, side, position].set(pair_slots.T)]
  transfers between devices with their start and end apart: 2 -> 1, of which waited for: 1 -> 1; matrix products, arithmetic and copies ran while one was open for 22% -> 0% of each run, Pallas kernels for 0% -> 0%
where the time goes in v1:
time: 147 us; the launch traced here: 146 us
  Pallas kernels  81.8 us (56%)
  waiting for transfers between devices  27.5 us (19%)
  blocking collectives  25.8 us (18%)
  starting transfers between devices  5.16 us (4%)
  local copies, waits for them, and re-layouts  3.19 us (2%)
  other arithmetic  1.6 us (1%)
    pallas_call x1, Pallas kernels, pair_products(): pl.pallas_call(pair_kernel, grid_spec=pltpu.PrefetchScalarGridSpec(num_sc...  62.3 us
    all_to_all x1, waiting for transfers between devices, shards(): lax.all_to_all(found, 'dev', split_axis=0, concat_axis=0, tiled=True)  27.5 us
    all_gather x1, blocking collectives, shards(): everyone = lax.all_gather(named, 'dev', axis=0, tiled=False)  25.8 us
    pallas_call x1, Pallas kernels, pick(): pl.pallas_call(pick_kernel, out_shape=jax.ShapeDtypeStruct((CL_DEV, 4, PT...  14.9 us
    all_to_all x1, starting transfers between devices, shards(): lax.all_to_all(found, 'dev', split_axis=0, concat_axis=0, tiled=True)  5.16 us
    pallas_call x1, Pallas kernels, reply(): pl.pallas_call(reply_kernel, grid_spec=pltpu.PrefetchScalarGridSpec(num_s...  4.6 us
  transfers between devices with their start and end apart: 1, of which 1 were waited for; matrix products, arithmetic and copies ran while one was open for 0% of the time, Pallas kernels for 0%

profile of v1, /device:TPU:1, one launch (start us, length us, event | category | flops | bytes accessed | tf_op | source)
XLA Modules:
  0.0 145.7 jit_solution(6906412600622194323)
XLA Ops:
  0.6 0.7 fusion.1
  1.3 25.8 %all-gather.1 = s32[32,4,32]{2,1,0:T(4,128)S(1)} all-gather(s32[1,4,32]{2,1,0:T(4,128)S(1)} %get-tuple-element.4), channel_id=2, replica_groups=mesh['leaf'=4,'dev'=32] {'dev'}, dimensions={0}, use_global_device_ids=true | all-gather | bytes 16896 | tf_op jit(solution)/shard_map/all_gather | solution.py:170
  27.2 0.4 reduce_window_sum.11
  27.6 0.1 multiply_reduce_fusion
  27.8 0.1 copy.23
  27.9 0.7 reshape.45.wanted_ref
  28.6 1.6 %copy.32 = f32[1,3,128,128]{3,2,1,0:T(8,128)} copy(f32[1,3,128,128]{3,1,2,0:T(4,128)} %bitcast.21) | data formatting | bytes 393216
  30.3 14.9 %pick.1.points_ref = f32[16,4,1024]{2,1,0:T(4,128)} custom-call(s32[128,128]{1,0:T(8,128)} %bitcast.22, f32[3,128,128]{2,1,0:T(8,128)} %bitcast.20, f32[128,128]{1,0:T(8,128)} %bitcast.23), custom_call_target="tpu_custom_call" | custom-call | tf_op jit(solution)/shard_map/pick/pallas_call | solution.py:58
  45.1 4.6 %reply.1 = f32[128,4,1024]{2,1,0:T(4,128)} custom-call(s32[128]{0:T(128)} %reshape.45.wanted_ref, f32[16,4,1024]{2,1,0:T(4,128)} %pick.1.points_ref), custom_call_target="tpu_custom_call" | custom-call | tf_op jit(solution)/shard_map/reply/pallas_call | solution.py:76
  49.7 5.2 %all-to-all-start = ((f32[32,4,4,1024]{3,2,1,0:T(4,128)}), f32[32,4,4,1024]{3,2,1,0:T(4,128)S(1)}, u32[]{:S(2)}, u32[]{:S(2)}) async-start(f32[32,4,4,1024]{3,2,1,0:T(4,128)} %bitcast.19), calls=%async_computation | async-start | bytes 4194304 | tf_op jit(solution)/shard_map/all_to_all | solution.py:182
  54.9 0.1 iota_compare_fusion.1
  55.0 0.2 convert_reduce_fusion
  55.2 0.1 add_add_fusion
  55.3 27.5 %all-to-all-done = f32[32,4,4,1024]{3,2,1,0:T(4,128)S(1)} async-done(((f32[32,4,4,1024]{3,2,1,0:T(4,128)}), f32[32,4,4,1024]{3,2,1,0:T(4,128)S(1)}, u32[]{:S(2)}, u32[]{:S(2)}) %all-to-all-start) | async-done | bytes 2097184 | tf_op jit(solution)/shard_map/all_to_all | solution.py:182
  82.7 0.0 copy-start
  82.7 0.7 copy-done
  83.4 62.3 %pairs.1 = (bf16[32,1024,128]{2,1,0:T(8,128)(2,1)}, bf16[32,128,1024]{2,1,0:T(8,128)(2,1)}) custom-call(s32[32]{0:T(128)S(1)} %get-tuple-element.7.row_at, s32[32]{0:T(128)S(1)} %get-tuple-element.6.col_at, s32[32]{0:T(128)S(1)} %copy-done, f32[128,4,1024]{2,1,0:T(4,128)S(1)} %bitcast.17, f32[128,4,1024]{2,1,0:T(4,128)S(1)} %bitcast.18, ...), custom_call_target="tpu_custom_call" | custom-call | tf_op jit(solution)/shard_map/pairs/pallas_call | solution.py:139
  (8 shorter events, 0.1 us)
Async XLA Ops:
  49.7 33.0 %all-to-all-start = ((f32[32,4,4,1024]{3,2,1,0:T(4,128)}), f32[32,4,4,1024]{3,2,1,0:T(4,128)S(1)}, u32[]{:S(2)}, u32[]{:S(2)}) async-start(f32[32,4,4,1024]{3,2,1,0:T(4,128)} %bitcast.19), calls=%async_computation | async-start | bytes 4194304 | tf_op jit(solution)/shard_map/all_to_all | solution.py:182
  82.7 0.7 copy-start

commit v2 on v1

v2 whole, which is shorter than its diff:
```python
import functools
import math

import jax
import jax.numpy as jnp
from jax import lax
from jax.experimental import pallas as pl
from jax.experimental.pallas import tpu as pltpu
from jax.sharding import PartitionSpec as P

PTS = 1024
RK = 128
BLK = 32
CL_DEV = 16

softening = 0.01
bf16 = jnp.bfloat16
f32 = jnp.float32


def contract(a, b, dim_a, dim_b):
    return lax.dot_general(a, b, (((dim_a,), (dim_b,)), ((), ())), preferred_element_type=f32)

LEVELS = 65535
PICK_UNROLL = 32


def pick_kernel(order_ref, coords_ref, weights_ref, out_ref, pack_ref):
    step = LEVELS / 4.0

    def fixed(value, low):
        return (value * step + (0.5 - low * step)).astype(jnp.int32)

    pack_ref[0] = (fixed(coords_ref[0], -2.0) << 16) | fixed(coords_ref[1], -2.0)
    pack_ref[1] = (fixed(coords_ref[2], -2.0) << 16) | fixed(weights_ref[...], 0.0)
    for cluster in range(CL_DEV):
        index = order_ref[cluster * 8 : cluster * 8 + 8, :]
        high = index >> 7
        low = index & 127

        def turn(number, picked):
            picked = list(picked)
            for inner in range(PICK_UNROLL):
                row = number * PICK_UNROLL + inner
                here = high == row
                for part in range(2):
                    line = jnp.broadcast_to(pack_ref[part, pl.ds(row, 1), :], (8, 128))
                    found = jnp.take_along_axis(line, low, axis=1, mode="promise_in_bounds")
                    picked[part] = jnp.where(here, found, picked[part])
            return tuple(picked)

        zero = jnp.zeros((8, 128), jnp.int32)
        picked = lax.fori_loop(0, 128 // PICK_UNROLL, turn, (zero, zero))
        values = []
        for part in range(2):
            values.append(((picked[part] >> 16) & LEVELS).astype(f32) * (1.0 / step) - 2.0)
            second = (picked[part] & LEVELS).astype(f32) * (1.0 / step)
            values.append(second - 2.0 if part == 0 else second)
        for part in range(4):
            for line in range(8):
                out_ref[cluster, part : part + 1, line * 128 : line * 128 + 128] = values[part][
                    line : line + 1, :
                ]


def pick(order, coords, weights):
    return pl.pallas_call(
        pick_kernel,
        out_shape=jax.ShapeDtypeStruct((CL_DEV, 4, PTS), f32),
        in_specs=[pl.BlockSpec(memory_space=pltpu.VMEM)] * 3,
        out_specs=pl.BlockSpec(memory_space=pltpu.VMEM),
        scratch_shapes=[pltpu.VMEM((2, 128, 128), jnp.int32)],
        cost_estimate=pl.CostEstimate(flops=40_000_000, bytes_accessed=600_000, transcendentals=0),
        name="pick",
    )(order, coords, weights)


def plan_kernel(named_ref, wanted_ref, places_ref):
    count = named_ref.shape[1]
    square = (count, count)
    named = named_ref[...].astype(f32)
    down = lax.broadcasted_iota(jnp.int32, square, 0)
    along = lax.broadcasted_iota(jnp.int32, square, 1)
    eye = down == along
    number = along.astype(f32)
    number_down = down.astype(f32)

    def column(row):
        return jnp.sum(jnp.where(eye, row, 0.0), axis=1, keepdims=True)

    def product(a, b):
        return jnp.where(contract(a, b, 1, 0) > 0.5, 1.0, 0.0).astype(bf16)

    row_owner, col_owner, row_slot, col_slot, rank = (named[i : i + 1] for i in range(5))
    same_row = jnp.where((column(row_owner) == row_owner) & ~eye, 1.0, 0.0)
    same_col = jnp.where((column(col_owner) == col_owner) & ~eye, 1.0, 0.0)
    either = (same_row + same_col).astype(bf16)
    same_row, same_col = same_row.astype(bf16), same_col.astype(bf16)
    steps = contract(same_row, same_col, 1, 0) + contract(same_col, same_row, 1, 0)
    alike = jnp.where(eye | (steps > 0.5), 1.0, 0.0).astype(bf16)
    for _ in range(4):
        alike = product(alike, alike)
    other = product(alike, either)
    far = float(2 * count)
    least = jnp.min(jnp.where(alike.astype(f32) > 0.5, number, far), axis=1, keepdims=True)
    least_other = jnp.min(jnp.where(other.astype(f32) > 0.5, number, far), axis=1, keepdims=True)
    first = jnp.where(least < least_other, 1.0, 0.0)
    size = jnp.sum(first, axis=0, keepdims=True)
    flip = size < count / 2
    first = jnp.where(flip, 1.0 - first, first)
    size = jnp.where(flip, count - size, size)
    first_row = jnp.sum(jnp.where(eye, first, 0.0), axis=0, keepdims=True)
    before = jnp.sum(jnp.where(along < down, first_row, 0.0), axis=1, keepdims=True)
    before_other = jnp.sum(jnp.where(along < down, 1.0 - first_row, 0.0), axis=1, keepdims=True)
    position = jnp.where(first > 0.5, before, size + before_other)
    hit = position == number

    def ordered(values):
        return jnp.sum(jnp.where(hit, values, 0.0), axis=0, keepdims=True)

    places = [
        ordered(number_down),
        ordered(column(row_owner * 2.0)),
        ordered(column(col_owner * 2.0 + 1.0)),
        ordered(column(rank)),
        ordered(1.0 - first),
    ]
    for line, value in enumerate(places):
        places_ref[line : line + 1, :] = value.astype(jnp.int32)
    places_ref[5:8, :] = jnp.zeros((3, count), jnp.int32)
    lane = lax.broadcasted_iota(jnp.int32, wanted_ref.shape, 1)
    wanted = jnp.zeros(wanted_ref.shape, f32)
    for phase in range(2):
        turn = first_row > 0.5 if phase == 0 else first_row < 0.5
        for side, (owner, slot) in enumerate(((row_owner, row_slot), (col_owner, col_slot))):
            value = jnp.sum(
                jnp.where((owner == number_down) & turn, slot, 0.0), axis=1, keepdims=True
            )
            wanted = jnp.where(lane == phase * 2 + side, value, wanted)
    wanted_ref[...] = wanted.astype(jnp.int32)


def plan(named, members):
    count = named.shape[1]
    return pl.pallas_call(
        plan_kernel,
        out_shape=[
            jax.ShapeDtypeStruct((members, 128), jnp.int32),
            jax.ShapeDtypeStruct((8, count), jnp.int32),
        ],
        in_specs=[pl.BlockSpec(memory_space=pltpu.VMEM)],
        out_specs=[pl.BlockSpec(memory_space=pltpu.VMEM)] * 2,
        name="plan",
    )(named)


def reply_kernel(phase, wanted_ref, points_ref, out_ref, sem):
    for member in range(out_ref.shape[0]):
        for side in range(2):
            pltpu.make_async_copy(
                points_ref.at[wanted_ref[member, phase * 2 + side]],
                out_ref.at[member, side],
                sem,
            ).start()
    pltpu.make_async_copy(out_ref, out_ref, sem).wait()


def reply(phase, wanted, points):
    members = wanted.shape[0]
    return pl.pallas_call(
        functools.partial(reply_kernel, phase),
        in_specs=[
            pl.BlockSpec(memory_space=pltpu.SMEM),
            pl.BlockSpec(memory_space=pltpu.VMEM),
        ],
        out_specs=pl.BlockSpec(memory_space=pltpu.HBM),
        out_shape=jax.ShapeDtypeStruct((members, 2, 4, PTS), f32),
        scratch_shapes=[pltpu.SemaphoreType.DMA],
        cost_estimate=pl.CostEstimate(flops=0, bytes_accessed=4_000_000, transcendentals=0),
        name="reply",
    )(wanted, points)


def split3(value):
    first = value.astype(bf16).astype(f32)
    rest = value - first
    second = rest.astype(bf16).astype(f32)
    return first, second, rest - second


def distance_operands(rows, cols):
    line = lax.broadcasted_iota(jnp.int32, (4, PTS), 0)
    row_square = rows[0:1] * rows[0:1] + rows[1:2] * rows[1:2] + rows[2:3] * rows[2:3]
    left = jnp.where(line < 3, rows, row_square)
    inverse = 1.0 / (cols[3:4] * cols[3:4])
    col_square = cols[0:1] * cols[0:1] + cols[1:2] * cols[1:2] + cols[2:3] * cols[2:3]
    right = jnp.where(line < 3, cols * (-2.0 * inverse), inverse)
    l1, l2, l3 = split3(left)
    r1, r2, r3 = split3(right)
    c1, c2, c3 = split3((col_square + softening) * inverse)
    ones = jnp.ones((4, PTS), f32)
    zero = jnp.zeros((4, PTS), f32)
    last = jnp.where(line == 0, c1, jnp.where(line == 1, c2, jnp.where(line == 2, c3, 0.0)))
    left = jnp.concatenate([l1, l1, l2, l1, l2, l3, ones, zero], axis=0).astype(bf16)
    right = jnp.concatenate([r1, r2, r1, r3, r2, r1, last, zero], axis=0).astype(bf16)
    return left, right


def pair_block(first, places, rows, cols, sketch_ref, range_ref, co_ref):
    left, right = distance_operands(rows, cols)
    limit = places[3, first + pl.program_id(0)] * BLK
    test = sketch_ref[0]
    active = lax.broadcasted_iota(jnp.int32, (1, RK), 1) < limit
    masked = jnp.where(active, test, jnp.zeros_like(test)).T
    block = lax.rsqrt(contract(right, left, 0, 0)).astype(bf16)
    ranged = contract(masked, block, 1, 0).astype(bf16)
    range_ref[0] = ranged.T
    co_ref[0] = (contract(ranged, block, 1, 1) * (1.0 / math.sqrt(PTS))).astype(bf16)


def early_kernel(places, rows_ref, cols_ref, sketch_ref, range_ref, co_ref):
    pair_block(0, places, rows_ref[0], cols_ref[0], sketch_ref, range_ref, co_ref)


def late_kernel(
    first, places, rows_0, cols_0, rows_1, cols_1, sketch_ref, old_range, old_co, range_ref, co_ref
):
    early = places[4, first + pl.program_id(0)] == 0
    rows = jnp.where(early, rows_0[0], rows_1[0])
    cols = jnp.where(early, cols_0[0], cols_1[0])
    pair_block(first, places, rows, cols, sketch_ref, range_ref, co_ref)


def pair_products(first, number, places, replies, sketch, old):
    count = sketch.shape[0]
    points = []
    for phase in range(len(replies)):
        for line in (1, 2):

            def at(p, places, phase=phase, line=line):
                place = places[line, first + p]
                if len(replies) > 1:
                    late = places[4, first + p]
                    place = place * (late if phase else 1 - late)
                return (place, 0, 0)

            points.append(pl.BlockSpec((1, 4, PTS), at))

    def own(p, places):
        return (places[0, first + p], 0, 0)

    pair_specs = [pl.BlockSpec((1, PTS, RK), own), pl.BlockSpec((1, RK, PTS), own)]
    operands = [places] + [reply for reply in replies for _ in range(2)] + [sketch] + list(old)
    body = functools.partial(late_kernel, first) if old else early_kernel
    return pl.pallas_call(
        body,
        grid_spec=pltpu.PrefetchScalarGridSpec(
            num_scalar_prefetch=1,
            grid=(number,),
            in_specs=points
            + pair_specs[:1]
            + [pl.BlockSpec(memory_space=pl.ANY) for _ in old],
            out_specs=pair_specs,
        ),
        out_shape=[
            jax.ShapeDtypeStruct((count, PTS, RK), bf16),
            jax.ShapeDtypeStruct((count, RK, PTS), bf16),
        ],
        input_output_aliases={len(operands) - 2: 0, len(operands) - 1: 1} if old else {},
        compiler_params=pltpu.CompilerParams(vmem_limit_bytes=48 << 20),
        cost_estimate=pl.CostEstimate(
            flops=number * 6 * PTS * PTS * 256, bytes_accessed=number * 800_000, transcendentals=0
        ),
        name="pairs",
    )(*operands)


def shards(
    panel_coords, panel_weights, panel_order, row_owner, col_owner, pair_slots, rank_blocks, sketch
):
    members = lax.axis_size("dev")
    count = rank_blocks.shape[0]
    named = jnp.concatenate(
        [row_owner, col_owner, pair_slots, rank_blocks[:, None], jnp.zeros((count, 3), jnp.int32)],
        axis=1,
    ).T
    wanted, places = plan(named, members)
    asked = lax.all_to_all(wanted, "dev", split_axis=0, concat_axis=0, tiled=True)
    points = pick(
        panel_order.reshape(128, 128),
        panel_coords.reshape(3, 128, 128),
        panel_weights.reshape(128, 128),
    )
    replies = []
    for phase in range(2):
        found = reply(phase, asked, points)
        got = lax.all_to_all(found, "dev", split_axis=0, concat_axis=0, tiled=True)
        replies.append(got.reshape(members * 2, 4, PTS))
    half = count // 2
    early = pair_products(0, half, places, replies[:1], sketch, ())
    return tuple(pair_products(half, count - half, places, replies, sketch, early))


def solution(mesh):
    in_specs = (
        P(None, ("leaf", "dev")),
        P(("leaf", "dev")),
        P(("leaf", "dev"), None),
        P(("leaf", "dev"), None),
        P(("leaf", "dev"), None),
        P(("leaf", "dev"), None),
        P(("leaf", "dev")),
        P(("leaf", "dev"), None, None),
    )
    out_specs = (P(("leaf", "dev"), None, None), P(("leaf", "dev"), None, None))
    return jax.shard_map(shards, mesh=mesh, in_specs=in_specs, out_specs=out_specs, check_vma=False)
```

time: 147 us -> 118 us (0.80)
  blocking collectives: 25.8 us -> 0 us
  starting transfers between devices: 5.16 us -> 20 us
  waiting for transfers between devices: 27.5 us -> 15.2 us
  Pallas kernels: 81.8 us -> 77.7 us
  other arithmetic: 1.6 us -> 0 us
    all_gather x1 -> x0, blocking collectives: 25.8 us -> none  [shards(): everyone = lax.all_gather(named, 'dev', axis=0, tiled=False)]
    all_to_all x1 -> x3, starting transfers between devices: 5.16 us -> 20 us  [the longest x2 11.4 us: shards(): got = lax.all_to_all(found, 'dev', split_axis=0, concat_axis=0, tiled=True)]
    all_to_all x1 -> x3, waiting for transfers between devices: 27.5 us -> 15.2 us  [the longest x2 15.2 us: shards(): got = lax.all_to_all(found, 'dev', split_axis=0, concat_axis=0, tiled=True)]
    pallas_call x1, Pallas kernels: 14.9 us -> 10.7 us  [pick(): pl.pallas_call(pick_kernel, out_shape=jax.ShapeDtypeStruct((CL_DEV, 4, PT...]
    pallas_call x2 -> x5, Pallas kernels: 66.9 us -> 67 us  [the longest x2 60.8 us: pair_products(): pl.pallas_call(body, grid_spec=pltpu.PrefetchScalarGridSpec(num_scalar_pr...]
  transfers between devices with their start and end apart: 1 -> 3, of which waited for: 1 -> 1; matrix products, arithmetic and copies ran while one was open for 0% -> 1% of each run, Pallas kernels for 0% -> 36%
where the time goes in v2:
time: 118 us
  Pallas kernels  77.7 us (66%)
  starting transfers between devices  20 us (17%)
  waiting for transfers between devices  15.2 us (13%)
  local copies, waits for them, and re-layouts  4.25 us (4%)
    pallas_call x2, Pallas kernels, pair_products(): pl.pallas_call(body, grid_spec=pltpu.PrefetchScalarGridSpec(num_scalar_pr...  60.8 us
    all_to_all x2, waiting for transfers between devices, shards(): got = lax.all_to_all(found, 'dev', split_axis=0, concat_axis=0, tiled=True)  15.2 us
    all_to_all x2, starting transfers between devices, shards(): got = lax.all_to_all(found, 'dev', split_axis=0, concat_axis=0, tiled=True)  11.4 us
    pallas_call x1, Pallas kernels, pick(): pl.pallas_call(pick_kernel, out_shape=jax.ShapeDtypeStruct((CL_DEV, 4, PT...  10.7 us
    all_to_all x1, starting transfers between devices, shards(): lax.all_to_all(wanted, 'dev', split_axis=0, concat_axis=0, tiled=True)  8.59 us
    pallas_call x2, Pallas kernels, reply(): pl.pallas_call(functools.partial(reply_kernel, phase), in_specs=[pl.Block...  3.85 us
    unnamed x7, local copies, waits for them, and re-layouts  2.93 us
  transfers between devices with their start and end apart: 3, of which 1 were waited for; matrix products, arithmetic and copies ran while one was open for 1% of the time, Pallas kernels for 36%

profile of v2, /device:TPU:1, one launch (start us, length us, event | category | flops | bytes accessed | tf_op | source)
XLA Modules:
  0.0 117.8 jit_solution(9830134064297060854)
XLA Ops:
  0.6 1.3 %concatenate.3 = s32[32,8]{0,1:T(8,128)} concatenate(s32[32,1]{0,1:T(1,128)} %param.11, s32[32,1]{0,1:T(1,128)} %param.12, s32[32,2]{0,1:T(2,128)} %param.13, s32[32,1]{0,1:T(1,128)} %bitcast.28, s32[32,3]{0,1:T(4,128)S(1)} %broadcast_in_dim.7), dimensions={1} | concatenate | bytes 2048 | tf_op jit(solution)/shard_map/concatenate | solution.py:283
  2.0 2.3 %plan.1 = (s32[32,128]{1,0:T(8,128)}, s32[8,32]{1,0:T(8,128)}) custom-call(s32[8,32]{1,0:T(8,128)} %bitcast.27), custom_call_target="tpu_custom_call" | custom-call | tf_op jit(solution)/shard_map/plan/pallas_call | solution.py:145
  4.3 8.6 %all-to-all-start = ((s32[32,1,128]{2,1,0:T(1,128)}), s32[32,1,128]{2,1,0:T(1,128)S(1)}, u32[]{:S(2)}, u32[]{:S(2)}) async-start(s32[32,1,128]{2,1,0:T(1,128)} %bitcast.26), calls=%async_computation | async-start | bytes 32768 | tf_op jit(solution)/shard_map/all_to_all | solution.py:288
  12.9 1.6 %copy.15 = f32[1,3,128,128]{3,2,1,0:T(8,128)} copy(f32[1,3,128,128]{3,1,2,0:T(4,128)} %bitcast.21) | data formatting | bytes 393216
  14.5 10.7 %pick.1.points_ref = f32[16,4,1024]{2,1,0:T(4,128)} custom-call(s32[128,128]{1,0:T(8,128)} %bitcast.24, f32[3,128,128]{2,1,0:T(8,128)} %bitcast.20, f32[128,128]{1,0:T(8,128)} %bitcast.25), custom_call_target="tpu_custom_call" | custom-call | flops 40000000 | bytes 600000 | tf_op jit(solution)/shard_map/pick/pallas_call | solution.py:67
  25.2 0.0 all-to-all-done
  25.2 0.0 copy-start.2
  25.2 0.6 copy-done.2
  25.8 1.9 %reply.2 = f32[32,2,4,1024]{3,2,1,0:T(4,128)} custom-call(s32[32,128]{1,0:T(8,128)} %bitcast.22, f32[16,4,1024]{2,1,0:T(4,128)} %pick.1.points_ref), custom_call_target="tpu_custom_call" | custom-call | bytes 4000000 | tf_op jit(solution)/shard_map/reply/pallas_call | solution.py:170
  27.7 7.4 %all-to-all-start.1 = ((f32[32,2,4,1024]{3,2,1,0:T(4,128)}), f32[32,2,4,1024]{3,2,1,0:T(4,128)S(1)}, u32[]{:S(2)}, u32[]{:S(2)}) async-start(f32[32,2,4,1024]{3,2,1,0:T(4,128)} %reply.2), calls=%async_computation.1 | async-start | bytes 2097152 | tf_op jit(solution)/shard_map/all_to_all | solution.py:297
  35.1 1.9 %reply.3 = f32[32,2,4,1024]{3,2,1,0:T(4,128)} custom-call(s32[32,128]{1,0:T(8,128)} %bitcast.23, f32[16,4,1024]{2,1,0:T(4,128)} %pick.1.points_ref), custom_call_target="tpu_custom_call" | custom-call | bytes 4000000 | tf_op jit(solution)/shard_map/reply/pallas_call | solution.py:170
  37.1 15.2 %all-to-all-done.1 = f32[32,2,4,1024]{3,2,1,0:T(4,128)S(1)} async-done(((f32[32,2,4,1024]{3,2,1,0:T(4,128)}), f32[32,2,4,1024]{3,2,1,0:T(4,128)S(1)}, u32[]{:S(2)}, u32[]{:S(2)}) %all-to-all-start.1) | async-done | bytes 1048608 | tf_op jit(solution)/shard_map/all_to_all | solution.py:297
  52.3 4.0 %all-to-all-start.2 = ((f32[32,2,4,1024]{3,2,1,0:T(4,128)}), f32[32,2,4,1024]{3,2,1,0:T(4,128)S(1)}, u32[]{:S(2)}, u32[]{:S(2)}) async-start(f32[32,2,4,1024]{3,2,1,0:T(4,128)} %reply.3), calls=%async_computation.2 | async-start | bytes 2097152 | tf_op jit(solution)/shard_map/all_to_all | solution.py:297
  56.3 0.0 copy-start
  56.3 0.7 copy-done
  57.0 0.0 copy-start.1
  57.0 30.3 %pairs.2 = (bf16[32,1024,128]{2,1,0:T(8,128)(2,1)}, bf16[32,128,1024]{2,1,0:T(8,128)(2,1)}) custom-call(s32[8,32]{1,0:T(8,128)S(1)} %copy-done, f32[64,4,1024]{2,1,0:T(4,128)S(1)} %bitcast.14, f32[64,4,1024]{2,1,0:T(4,128)S(1)} %bitcast.15, bf16[32,1024,128]{2,1,0:T(8,128)(2,1)} %sketch_ref.3), custom_call_target="tpu_custom_call" | custom-call | flops 25769803776 | bytes 12800000 | tf_op jit(solution)/shard_map/pairs/pallas_call | solution.py:255
  87.3 0.0 all-to-all-done.2
  87.3 0.0 copy-done.1
  87.3 30.5 %pairs.3 = (bf16[32,1024,128]{2,1,0:T(8,128)(2,1)}, bf16[32,128,1024]{2,1,0:T(8,128)(2,1)}) custom-call(s32[8,32]{1,0:T(8,128)S(1)} %copy-done.1, f32[64,4,1024]{2,1,0:T(4,128)S(1)} %bitcast.16, f32[64,4,1024]{2,1,0:T(4,128)S(1)} %bitcast.17, f32[64,4,1024]{2,1,0:T(4,128)S(1)} %bitcast.18, ...), custom_call_target="tpu_custom_call", output_to_operand_aliasing={{0}: (6, {}), {1}: (7, {})} | custom-call | flops 25769803776 | bytes 12800000 | tf_op jit(solution)/shard_map/pairs/pallas_call | solution.py:255
  (1 shorter events, 0.0 us)
Async XLA Ops:
  4.3 20.9 %all-to-all-start = ((s32[32,1,128]{2,1,0:T(1,128)}), s32[32,1,128]{2,1,0:T(1,128)S(1)}, u32[]{:S(2)}, u32[]{:S(2)}) async-start(s32[32,1,128]{2,1,0:T(1,128)} %bitcast.26), calls=%async_computation | async-start | bytes 32768 | tf_op jit(solution)/shard_map/all_to_all | solution.py:288
  25.2 0.6 copy-start.2
  27.7 24.6 %all-to-all-start.1 = ((f32[32,2,4,1024]{3,2,1,0:T(4,128)}), f32[32,2,4,1024]{3,2,1,0:T(4,128)S(1)}, u32[]{:S(2)}, u32[]{:S(2)}) async-start(f32[32,2,4,1024]{3,2,1,0:T(4,128)} %reply.2), calls=%async_computation.1 | async-start | bytes 2097152 | tf_op jit(solution)/shard_map/all_to_all | solution.py:297
  52.3 34.9 %all-to-all-start.2 = ((f32[32,2,4,1024]{3,2,1,0:T(4,128)}), f32[32,2,4,1024]{3,2,1,0:T(4,128)S(1)}, u32[]{:S(2)}, u32[]{:S(2)}) async-start(f32[32,2,4,1024]{3,2,1,0:T(4,128)} %reply.3), calls=%async_computation.2 | async-start | bytes 2097152 | tf_op jit(solution)/shard_map/all_to_all | solution.py:297
  56.3 0.7 copy-start
  57.0 30.3 %copy-start.1 = (s32[8,32]{1,0:T(8,128)S(1)}, s32[8,32]{1,0:T(8,128)}, u32[]{:S(2)}) copy-start(s32[8,32]{1,0:T(8,128)} %get-tuple-element.6.places) | copy-start | bytes 3076

commit v3 on v2

--- a/solution.py
+++ b/solution.py
@@ -21,46 +21,45 @@
 def contract(a, b, dim_a, dim_b):
     return lax.dot_general(a, b, (((dim_a,), (dim_b,)), ((), ())), preferred_element_type=f32)
 
-LEVELS = 65535
-PICK_UNROLL = 32
-
-
-def pick_kernel(order_ref, coords_ref, weights_ref, out_ref, pack_ref):
-    step = LEVELS / 4.0
-
-    def fixed(value, low):
-        return (value * step + (0.5 - low * step)).astype(jnp.int32)
-
-    pack_ref[0] = (fixed(coords_ref[0], -2.0) << 16) | fixed(coords_ref[1], -2.0)
-    pack_ref[1] = (fixed(coords_ref[2], -2.0) << 16) | fixed(weights_ref[...], 0.0)
-    for cluster in range(CL_DEV):
-        index = order_ref[cluster * 8 : cluster * 8 + 8, :]
-        high = index >> 7
-        low = index & 127
-
-        def turn(number, picked):
-            picked = list(picked)
-            for inner in range(PICK_UNROLL):
-                row = number * PICK_UNROLL + inner
-                here = high == row
-                for part in range(2):
-                    line = jnp.broadcast_to(pack_ref[part, pl.ds(row, 1), :], (8, 128))
-                    found = jnp.take_along_axis(line, low, axis=1, mode="promise_in_bounds")
-                    picked[part] = jnp.where(here, found, picked[part])
-            return tuple(picked)
-
-        zero = jnp.zeros((8, 128), jnp.int32)
-        picked = lax.fori_loop(0, 128 // PICK_UNROLL, turn, (zero, zero))
-        values = []
-        for part in range(2):
-            values.append(((picked[part] >> 16) & LEVELS).astype(f32) * (1.0 / step) - 2.0)
-            second = (picked[part] & LEVELS).astype(f32) * (1.0 / step)
-            values.append(second - 2.0 if part == 0 else second)
+PICK_TURN = 2
+LANES = 256
+
+
+def pick_kernel(order_ref, coords_ref, weights_ref, out_ref, table_ref, split_ref):
+    for part in range(3):
+        for m in range(64):
+            table_ref[part * 64 + m : part * 64 + m + 1, :] = coords_ref[
+                part : part + 1, m * 256 : m * 256 + 256
+            ]
+    for half in range(2):
+        table_ref[192:256, half * 128 : half * 128 + 128] = weights_ref[
+            pl.ds(half, 64, stride=2), :
+        ]
+    table = table_ref[...]
+    head = table.astype(bf16)
+    split_ref[:, 0:256] = head
+    split_ref[:, 256:512] = (table - head.astype(f32)).astype(bf16)
+
+    def some_points(cluster, lane):
+        index = order_ref[0:1, pl.ds(pl.multiple_of(cluster * PTS + lane, LANES), LANES)]
+        k = lax.broadcasted_iota(jnp.int32, (256, LANES), 0)
+        hot = jnp.where(k == (index & 255), 1.0, 0.0).astype(bf16)
+        found = contract(split_ref[...], jnp.concatenate([hot, hot], axis=0), 1, 0)
+        m = lax.broadcasted_iota(jnp.int32, (64, LANES), 0)
+        here = m == (index >> 8)
         for part in range(4):
-            for line in range(8):
-                out_ref[cluster, part : part + 1, line * 128 : line * 128 + 128] = values[part][
-                    line : line + 1, :
-                ]
+            rows = found[part * 64 : part * 64 + 64]
+            out_ref[cluster, part : part + 1, lane : lane + LANES] = jnp.sum(
+                jnp.where(here, rows, 0.0), axis=0, keepdims=True
+            )
+
+    def turn(number, carry):
+        for inner in range(PICK_TURN):
+            for lane in range(0, PTS, LANES):
+                some_points(number * PICK_TURN + inner, lane)
+        return carry
+
+    lax.fori_loop(0, CL_DEV // PICK_TURN, turn, 0)
 
 
 def pick(order, coords, weights):
@@ -69,16 +68,21 @@
         out_shape=jax.ShapeDtypeStruct((CL_DEV, 4, PTS), f32),
         in_specs=[pl.BlockSpec(memory_space=pltpu.VMEM)] * 3,
         out_specs=pl.BlockSpec(memory_space=pltpu.VMEM),
-        scratch_shapes=[pltpu.VMEM((2, 128, 128), jnp.int32)],
-        cost_estimate=pl.CostEstimate(flops=40_000_000, bytes_accessed=600_000, transcendentals=0),
+        scratch_shapes=[pltpu.VMEM((256, 256), f32), pltpu.VMEM((256, 512), bf16)],
+        compiler_params=pltpu.CompilerParams(vmem_limit_bytes=32 << 20),
+        cost_estimate=pl.CostEstimate(
+            flops=5_000_000_000, bytes_accessed=600_000, transcendentals=0
+        ),
         name="pick",
     )(order, coords, weights)
 
 
-def plan_kernel(named_ref, wanted_ref, places_ref):
-    count = named_ref.shape[1]
+def plan_kernel(row_ref, col_ref, slots_ref, rank_ref, wanted_ref, places_ref):
+    count = rank_ref.shape[1]
     square = (count, count)
-    named = named_ref[...].astype(f32)
+    row_owner, col_owner = row_ref[...].astype(f32), col_ref[...].astype(f32)
+    row_slot, col_slot = slots_ref[0:1, :].astype(f32), slots_ref[1:2, :].astype(f32)
+    rank = rank_ref[...].astype(f32)
     down = lax.broadcasted_iota(jnp.int32, square, 0)
     along = lax.broadcasted_iota(jnp.int32, square, 1)
     eye = down == along
@@ -91,7 +95,6 @@
     def product(a, b):
         return jnp.where(contract(a, b, 1, 0) > 0.5, 1.0, 0.0).astype(bf16)
 
-    row_owner, col_owner, row_slot, col_slot, rank = (named[i : i + 1] for i in range(5))
     same_row = jnp.where((column(row_owner) == row_owner) & ~eye, 1.0, 0.0)
     same_col = jnp.where((column(col_owner) == col_owner) & ~eye, 1.0, 0.0)
     either = (same_row + same_col).astype(bf16)
@@ -140,18 +143,18 @@
     wanted_ref[...] = wanted.astype(jnp.int32)
 
 
-def plan(named, members):
-    count = named.shape[1]
+def plan(row_owner, col_owner, slots, rank, members):
+    count = rank.shape[1]
     return pl.pallas_call(
         plan_kernel,
         out_shape=[
             jax.ShapeDtypeStruct((members, 128), jnp.int32),
             jax.ShapeDtypeStruct((8, count), jnp.int32),
         ],
-        in_specs=[pl.BlockSpec(memory_space=pltpu.VMEM)],
+        in_specs=[pl.BlockSpec(memory_space=pltpu.VMEM)] * 4,
         out_specs=[pl.BlockSpec(memory_space=pltpu.VMEM)] * 2,
         name="plan",
-    )(named)
+    )(row_owner, col_owner, slots, rank)
 
 
 def reply_kernel(phase, wanted_ref, points_ref, out_ref, sem):
@@ -206,61 +209,62 @@
     return left, right
 
 
-def pair_block(first, places, rows, cols, sketch_ref, range_ref, co_ref):
-    left, right = distance_operands(rows, cols)
-    limit = places[3, first + pl.program_id(0)] * BLK
+def pair_kernel(first, number, phases, places, *refs):
+    replies = refs[:phases]
+    sketch_ref = refs[phases]
+    range_ref, co_ref, turned_ref, left_ref, right_ref = refs[-5:]
+    p = pl.program_id(0)
+
+    def prepare(pair, slot):
+        row_at, col_at = places[1, pair], places[2, pair]
+        rows, cols = replies[0][row_at], replies[0][col_at]
+        if phases > 1:
+            early = places[4, pair] == 0
+            rows = jnp.where(early, rows, replies[1][row_at])
+            cols = jnp.where(early, cols, replies[1][col_at])
+        left, right = distance_operands(rows, cols)
+        left_ref[slot] = left
+        right_ref[slot] = right.T
+
+    @pl.when(p == 0)
+    def _():
+        prepare(first, 0)
+
+    slot = lax.rem(p, 2)
+    limit = places[3, first + p] * BLK
     test = sketch_ref[0]
     active = lax.broadcasted_iota(jnp.int32, (1, RK), 1) < limit
     masked = jnp.where(active, test, jnp.zeros_like(test)).T
-    block = lax.rsqrt(contract(right, left, 0, 0)).astype(bf16)
+    block = lax.rsqrt(contract(right_ref[slot], left_ref[slot], 1, 0)).astype(bf16)
+    prepare(first + jnp.minimum(p + 1, number - 1), 1 - slot)
     ranged = contract(masked, block, 1, 0).astype(bf16)
     range_ref[0] = ranged.T
-    co_ref[0] = (contract(ranged, block, 1, 1) * (1.0 / math.sqrt(PTS))).astype(bf16)
-
-
-def early_kernel(places, rows_ref, cols_ref, sketch_ref, range_ref, co_ref):
-    pair_block(0, places, rows_ref[0], cols_ref[0], sketch_ref, range_ref, co_ref)
-
-
-def late_kernel(
-    first, places, rows_0, cols_0, rows_1, cols_1, sketch_ref, old_range, old_co, range_ref, co_ref
-):
-    early = places[4, first + pl.program_id(0)] == 0
-    rows = jnp.where(early, rows_0[0], rows_1[0])
-    cols = jnp.where(early, cols_0[0], cols_1[0])
-    pair_block(first, places, rows, cols, sketch_ref, range_ref, co_ref)
+    turned_ref[...] = block.T
+    co_ref[0] = (contract(ranged, turned_ref[...], 1, 0) * (1.0 / math.sqrt(PTS))).astype(bf16)
 
 
 def pair_products(first, number, places, replies, sketch, old):
     count = sketch.shape[0]
-    points = []
-    for phase in range(len(replies)):
-        for line in (1, 2):
-
-            def at(p, places, phase=phase, line=line):
-                place = places[line, first + p]
-                if len(replies) > 1:
-                    late = places[4, first + p]
-                    place = place * (late if phase else 1 - late)
-                return (place, 0, 0)
-
-            points.append(pl.BlockSpec((1, 4, PTS), at))
 
     def own(p, places):
         return (places[0, first + p], 0, 0)
 
     pair_specs = [pl.BlockSpec((1, PTS, RK), own), pl.BlockSpec((1, RK, PTS), own)]
-    operands = [places] + [reply for reply in replies for _ in range(2)] + [sketch] + list(old)
-    body = functools.partial(late_kernel, first) if old else early_kernel
+    operands = [places] + list(replies) + [sketch] + list(old)
     return pl.pallas_call(
-        body,
+        functools.partial(pair_kernel, first, number, len(replies)),
         grid_spec=pltpu.PrefetchScalarGridSpec(
             num_scalar_prefetch=1,
             grid=(number,),
-            in_specs=points
+            in_specs=[pl.BlockSpec(memory_space=pltpu.VMEM) for _ in replies]
             + pair_specs[:1]
             + [pl.BlockSpec(memory_space=pl.ANY) for _ in old],
             out_specs=pair_specs,
+            scratch_shapes=[
+                pltpu.VMEM((PTS, PTS), bf16),
+                pltpu.VMEM((2, 32, PTS), bf16),
+                pltpu.VMEM((2, PTS, 32), bf16),
+            ],
         ),
         out_shape=[
             jax.ShapeDtypeStruct((count, PTS, RK), bf16),
@@ -280,17 +284,15 @@
 ):
     members = lax.axis_size("dev")
     count = rank_blocks.shape[0]
-    named = jnp.concatenate(
-        [row_owner, col_owner, pair_slots, rank_blocks[:, None], jnp.zeros((count, 3), jnp.int32)],
-        axis=1,
-    ).T
-    wanted, places = plan(named, members)
+    wanted, places = plan(
+        row_owner.reshape(1, count),
+        col_owner.reshape(1, count),
+        pair_slots.T,
+        rank_blocks.reshape(1, count),
+        members,
+    )
     asked = lax.all_to_all(wanted, "dev", split_axis=0, concat_axis=0, tiled=True)
-    points = pick(
-        panel_order.reshape(128, 128),
-        panel_coords.reshape(3, 128, 128),
-        panel_weights.reshape(128, 128),
-    )
+    points = pick(panel_order, panel_coords, panel_weights.reshape(128, 128))
     replies = []
     for phase in range(2):
         found = reply(phase, asked, points)

time: 118 us -> 108 us (0.915)
  Pallas kernels: 77.7 us -> 67.5 us
    pallas_call x2, Pallas kernels: 60.8 us -> 53.5 us  [pair_products(): pl.pallas_call(functools.partial(pair_kernel, first, number, len(replies)...]
    pallas_call x1, Pallas kernels: 10.7 us -> 7.8 us  [pick(): pl.pallas_call(pick_kernel, out_shape=jax.ShapeDtypeStruct((CL_DEV, 4, PT...]
    concatenate x1 -> x0, local copies, waits for them, and re-layouts: 1.32 us -> none  [shards(): jnp.concatenate([row_owner, col_owner, pair_slots, rank_blocks[:, None],...]
    unnamed x7 -> x12, local copies, waits for them, and re-layouts: 2.93 us -> 3.93 us
  transfers between devices with their start and end apart: 3 -> 3, of which waited for: 1 -> 1; matrix products, arithmetic and copies ran while one was open for 1% -> 0% of each run, Pallas kernels for 36% -> 34%
where the time goes in v3:
time: 108 us; the launch traced here: 107 us
  Pallas kernels  67.5 us (62%)
  starting transfers between devices  20 us (19%)
  waiting for transfers between devices  15.2 us (14%)
  local copies, waits for them, and re-layouts  3.93 us (4%)
    pallas_call x2, Pallas kernels, pair_products(): pl.pallas_call(functools.partial(pair_kernel, first, number, len(replies)...  53.5 us
    all_to_all x2, waiting for transfers between devices, shards(): got = lax.all_to_all(found, 'dev', split_axis=0, concat_axis=0, tiled=True)  15.2 us
    all_to_all x2, starting transfers between devices, shards(): got = lax.all_to_all(found, 'dev', split_axis=0, concat_axis=0, tiled=True)  11.4 us
    all_to_all x1, starting transfers between devices, shards(): lax.all_to_all(wanted, 'dev', split_axis=0, concat_axis=0, tiled=True)  8.59 us
    pallas_call x1, Pallas kernels, pick(): pl.pallas_call(pick_kernel, out_shape=jax.ShapeDtypeStruct((CL_DEV, 4, PT...  7.8 us
    unnamed x12, local copies, waits for them, and re-layouts  3.93 us
    pallas_call x2, Pallas kernels, reply(): pl.pallas_call(functools.partial(reply_kernel, phase), in_specs=[pl.Block...  3.84 us
    pallas_call x1, Pallas kernels, plan(): pl.pallas_call(plan_kernel, out_shape=[jax.ShapeDtypeStruct((members, 128...  2.33 us
  transfers between devices with their start and end apart: 3, of which 1 were waited for; matrix products, arithmetic and copies ran while one was open for 0% of the time, Pallas kernels for 34%

profile of v3, /device:TPU:1, one launch (start us, length us, event | category | flops | bytes accessed | tf_op | source)
XLA Modules:
  0.0 107.3 jit_solution(8523352106533571229)
XLA Ops:
  0.6 2.3 %plan.1 = (s32[32,128]{1,0:T(8,128)}, s32[8,32]{1,0:T(8,128)}) custom-call(s32[1,32]{1,0:T(1,128)} %bitcast.19, s32[1,32]{1,0:T(1,128)} %bitcast.20, s32[2,32]{1,0:T(2,128)} %bitcast.18, s32[1,32]{1,0:T(1,128)} %bitcast.21), custom_call_target="tpu_custom_call" | custom-call | tf_op jit(solution)/shard_map/plan/pallas_call | solution.py:148
  3.0 8.6 %all-to-all-start = ((s32[32,1,128]{2,1,0:T(1,128)}), s32[32,1,128]{2,1,0:T(1,128)S(1)}, u32[]{:S(2)}, u32[]{:S(2)}) async-start(s32[32,1,128]{2,1,0:T(1,128)} %bitcast.17), calls=%async_computation | async-start | bytes 32768 | tf_op jit(solution)/shard_map/all_to_all | solution.py:294
  11.6 0.0 copy-start.1
  11.6 0.9 copy-done.1
  12.5 0.0 copy-start.2
  12.5 0.8 copy-done.2
  13.4 0.0 copy-start.3
  13.4 0.8 copy-done.3
  14.2 0.0 copy-start.4
  14.2 7.8 %pick.1.points_ref = f32[16,4,1024]{2,1,0:T(4,128)S(1)} custom-call(s32[1,16384]{1,0:T(1,128)S(1)} %copy-done.2, f32[3,16384]{1,0:T(4,128)S(1)} %copy-done.1, f32[128,128]{1,0:T(8,128)S(1)} %bitcast.14), custom_call_target="tpu_custom_call" | custom-call | flops 5000000000 | bytes 600000 | tf_op jit(solution)/shard_map/pick/pallas_call | solution.py:66
  22.0 0.0 copy-start
  22.0 0.7 copy-done
  22.7 0.0 all-to-all-done
  22.7 0.0 copy-start.5
  22.7 0.6 copy-done.5
  23.3 1.9 %reply.2 = f32[32,2,4,1024]{3,2,1,0:T(4,128)} custom-call(s32[32,128]{1,0:T(8,128)} %bitcast.15, f32[16,4,1024]{2,1,0:T(4,128)} %copy-done), custom_call_target="tpu_custom_call" | custom-call | bytes 4000000 | tf_op jit(solution)/shard_map/reply/pallas_call | solution.py:173
  25.2 7.4 %all-to-all-start.1 = ((f32[32,2,4,1024]{3,2,1,0:T(4,128)}), f32[32,2,4,1024]{3,2,1,0:T(4,128)S(1)}, u32[]{:S(2)}, u32[]{:S(2)}) async-start(f32[32,2,4,1024]{3,2,1,0:T(4,128)} %reply.2), calls=%async_computation.1 | async-start | bytes 2097152 | tf_op jit(solution)/shard_map/all_to_all | solution.py:299
  32.6 1.9 %reply.3 = f32[32,2,4,1024]{3,2,1,0:T(4,128)} custom-call(s32[32,128]{1,0:T(8,128)} %bitcast.16, f32[16,4,1024]{2,1,0:T(4,128)} %copy-done), custom_call_target="tpu_custom_call" | custom-call | bytes 4000000 | tf_op jit(solution)/shard_map/reply/pallas_call | solution.py:173
  34.6 15.2 %all-to-all-done.1 = f32[32,2,4,1024]{3,2,1,0:T(4,128)S(1)} async-done(((f32[32,2,4,1024]{3,2,1,0:T(4,128)}), f32[32,2,4,1024]{3,2,1,0:T(4,128)S(1)}, u32[]{:S(2)}, u32[]{:S(2)}) %all-to-all-start.1) | async-done | bytes 1048608 | tf_op jit(solution)/shard_map/all_to_all | solution.py:299
  49.8 4.0 %all-to-all-start.2 = ((f32[32,2,4,1024]{3,2,1,0:T(4,128)}), f32[32,2,4,1024]{3,2,1,0:T(4,128)S(1)}, u32[]{:S(2)}, u32[]{:S(2)}) async-start(f32[32,2,4,1024]{3,2,1,0:T(4,128)} %reply.3), calls=%async_computation.2 | async-start | bytes 2097152 | tf_op jit(solution)/shard_map/all_to_all | solution.py:299
  53.8 0.0 copy-done.4
  53.8 26.5 %pairs.2 = (bf16[32,1024,128]{2,1,0:T(8,128)(2,1)}, bf16[32,128,1024]{2,1,0:T(8,128)(2,1)}) custom-call(s32[8,32]{1,0:T(8,128)S(1)} %copy-done.4, f32[64,4,1024]{2,1,0:T(4,128)S(1)} %bitcast.11, bf16[32,1024,128]{2,1,0:T(8,128)(2,1)} %refs_2_.1), custom_call_target="tpu_custom_call" | custom-call | flops 25769803776 | bytes 12800000 | tf_op jit(solution)/shard_map/pairs/pallas_call | solution.py:254
  80.3 0.0 all-to-all-done.2
  80.3 27.0 %pairs.3 = (bf16[32,1024,128]{2,1,0:T(8,128)(2,1)}, bf16[32,128,1024]{2,1,0:T(8,128)(2,1)}) custom-call(s32[8,32]{1,0:T(8,128)S(1)} %copy-done.4, f32[64,4,1024]{2,1,0:T(4,128)S(1)} %bitcast.12, f32[64,4,1024]{2,1,0:T(4,128)S(1)} %bitcast.13, bf16[32,1024,128]{2,1,0:T(8,128)(2,1)} %refs_2_.1, ...), custom_call_target="tpu_custom_call", output_to_operand_aliasing={{0}: (4, {}), {1}: (5, {})} | custom-call | flops 25769803776 | bytes 12800000 | tf_op jit(solution)/shard_map/pairs/pallas_call | solution.py:254
Async XLA Ops:
  3.0 19.8 %all-to-all-start = ((s32[32,1,128]{2,1,0:T(1,128)}), s32[32,1,128]{2,1,0:T(1,128)S(1)}, u32[]{:S(2)}, u32[]{:S(2)}) async-start(s32[32,1,128]{2,1,0:T(1,128)} %bitcast.17), calls=%async_computation | async-start | bytes 32768 | tf_op jit(solution)/shard_map/all_to_all | solution.py:294
  11.6 1.0 copy-start.1
  12.5 0.8 copy-start.2
  13.4 0.8 copy-start.3
  14.2 39.6 %copy-start.4 = (s32[8,32]{1,0:T(8,128)S(1)}, s32[8,32]{1,0:T(8,128)}, u32[]{:S(2)}) copy-start(s32[8,32]{1,0:T(8,128)} %get-tuple-element.6.places) | copy-start | bytes 3076
  22.0 0.7 copy-start
  22.7 0.6 copy-start.5
  25.2 24.6 %all-to-all-start.1 = ((f32[32,2,4,1024]{3,2,1,0:T(4,128)}), f32[32,2,4,1024]{3,2,1,0:T(4,128)S(1)}, u32[]{:S(2)}, u32[]{:S(2)}) async-start(f32[32,2,4,1024]{3,2,1,0:T(4,128)} %reply.2), calls=%async_computation.1 | async-start | bytes 2097152 | tf_op jit(solution)/shard_map/all_to_all | solution.py:299
  49.8 30.5 %all-to-all-start.2 = ((f32[32,2,4,1024]{3,2,1,0:T(4,128)}), f32[32,2,4,1024]{3,2,1,0:T(4,128)S(1)}, u32[]{:S(2)}, u32[]{:S(2)}) async-start(f32[32,2,4,1024]{3,2,1,0:T(4,128)} %reply.3), calls=%async_computation.2 | async-start | bytes 2097152 | tf_op jit(solution)/shard_map/all_to_all | solution.py:299

commit v4 on v3

--- a/solution.py
+++ b/solution.py
@@ -12,6 +12,7 @@
 RK = 128
 BLK = 32
 CL_DEV = 16
+CHUNK = 256
 
 softening = 0.01
 bf16 = jnp.bfloat16
@@ -25,12 +26,42 @@
 LANES = 256
 
 
-def pick_kernel(order_ref, coords_ref, weights_ref, out_ref, table_ref, split_ref):
+def pick_kernel(
+    asked_ref,
+    order_hbm,
+    coords_hbm,
+    weights_hbm,
+    out_ref,
+    found_ref,
+    order_ref,
+    coords_ref,
+    weights_ref,
+    asked_smem,
+    table_ref,
+    split_ref,
+    sems,
+    found_sem,
+):
+    fetches = [
+        pltpu.make_async_copy(source, target, sems.at[i])
+        for i, (source, target) in enumerate(
+            (
+                (coords_hbm, coords_ref),
+                (weights_hbm, weights_ref),
+                (order_hbm, order_ref),
+                (asked_ref, asked_smem),
+            )
+        )
+    ]
+    for fetch in fetches:
+        fetch.start()
+    fetches[0].wait()
     for part in range(3):
         for m in range(64):
             table_ref[part * 64 + m : part * 64 + m + 1, :] = coords_ref[
                 part : part + 1, m * 256 : m * 256 + 256
             ]
+    fetches[1].wait()
     for half in range(2):
         table_ref[192:256, half * 128 : half * 128 + 128] = weights_ref[
             pl.ds(half, 64, stride=2), :
@@ -39,6 +70,8 @@
     head = table.astype(bf16)
     split_ref[:, 0:256] = head
     split_ref[:, 256:512] = (table - head.astype(f32)).astype(bf16)
+
+    fetches[2].wait()
 
     def some_points(cluster, lane):
         index = order_ref[0:1, pl.ds(pl.multiple_of(cluster * PTS + lane, LANES), LANES)]
@@ -60,21 +93,51 @@
         return carry
 
     lax.fori_loop(0, CL_DEV // PICK_TURN, turn, 0)
-
-
-def pick(order, coords, weights):
+    fetches[3].wait()
+    send_found(0, asked_smem, out_ref, found_ref, found_sem)
+
+
+def send_found(phase, asked_smem, points_ref, found_ref, sem):
+    for member in range(found_ref.shape[0]):
+        for side in range(2):
+            pltpu.make_async_copy(
+                points_ref.at[asked_smem[member, phase * 2 + side]],
+                found_ref.at[member, side],
+                sem,
+            ).start()
+    pltpu.make_async_copy(found_ref, found_ref, sem).wait()
+
+
+def pick(asked, order, coords, weights):
+    members = asked.shape[0]
     return pl.pallas_call(
         pick_kernel,
-        out_shape=jax.ShapeDtypeStruct((CL_DEV, 4, PTS), f32),
-        in_specs=[pl.BlockSpec(memory_space=pltpu.VMEM)] * 3,
-        out_specs=pl.BlockSpec(memory_space=pltpu.VMEM),
-        scratch_shapes=[pltpu.VMEM((256, 256), f32), pltpu.VMEM((256, 512), bf16)],
-        compiler_params=pltpu.CompilerParams(vmem_limit_bytes=32 << 20),
+        out_shape=[
+            jax.ShapeDtypeStruct((CL_DEV, 4, PTS), f32),
+            jax.ShapeDtypeStruct((members, 2, 4, PTS), f32),
+        ],
+        in_specs=[pl.BlockSpec(memory_space=pltpu.VMEM)]
+        + [pl.BlockSpec(memory_space=pltpu.HBM)] * 3,
+        out_specs=[
+            pl.BlockSpec(memory_space=pltpu.VMEM),
+            pl.BlockSpec(memory_space=pltpu.HBM),
+        ],
+        scratch_shapes=[
+            pltpu.VMEM(order.shape, jnp.int32),
+            pltpu.VMEM(coords.shape, f32),
+            pltpu.VMEM(weights.shape, f32),
+            pltpu.SMEM(asked.shape, jnp.int32),
+            pltpu.VMEM((256, 256), f32),
+            pltpu.VMEM((256, 512), bf16),
+            pltpu.SemaphoreType.DMA((4,)),
+            pltpu.SemaphoreType.DMA,
+        ],
+        compiler_params=pltpu.CompilerParams(vmem_limit_bytes=56 << 20),
         cost_estimate=pl.CostEstimate(
-            flops=5_000_000_000, bytes_accessed=600_000, transcendentals=0
+            flops=5_000_000_000, bytes_accessed=4_000_000, transcendentals=0
         ),
         name="pick",
-    )(order, coords, weights)
+    )(asked, order, coords, weights)
 
 
 def plan_kernel(row_ref, col_ref, slots_ref, rank_ref, wanted_ref, places_ref):
@@ -157,31 +220,27 @@
     )(row_owner, col_owner, slots, rank)
 
 
-def reply_kernel(phase, wanted_ref, points_ref, out_ref, sem):
-    for member in range(out_ref.shape[0]):
-        for side in range(2):
-            pltpu.make_async_copy(
-                points_ref.at[wanted_ref[member, phase * 2 + side]],
-                out_ref.at[member, side],
-                sem,
-            ).start()
-    pltpu.make_async_copy(out_ref, out_ref, sem).wait()
-
-
-def reply(phase, wanted, points):
-    members = wanted.shape[0]
+def reply_kernel(asked_ref, points_ref, found_ref, asked_smem, asked_sem, sem):
+    fetch = pltpu.make_async_copy(asked_ref, asked_smem, asked_sem)
+    fetch.start()
+    fetch.wait()
+    send_found(1, asked_smem, points_ref, found_ref, sem)
+
+
+def reply(asked, points):
     return pl.pallas_call(
-        functools.partial(reply_kernel, phase),
-        in_specs=[
-            pl.BlockSpec(memory_space=pltpu.SMEM),
-            pl.BlockSpec(memory_space=pltpu.VMEM),
-        ],
+        reply_kernel,
+        in_specs=[pl.BlockSpec(memory_space=pltpu.VMEM)] * 2,
         out_specs=pl.BlockSpec(memory_space=pltpu.HBM),
-        out_shape=jax.ShapeDtypeStruct((members, 2, 4, PTS), f32),
-        scratch_shapes=[pltpu.SemaphoreType.DMA],
+        out_shape=jax.ShapeDtypeStruct((asked.shape[0], 2, 4, PTS), f32),
+        scratch_shapes=[
+            pltpu.SMEM(asked.shape, jnp.int32),
+            pltpu.SemaphoreType.DMA,
+            pltpu.SemaphoreType.DMA,
+        ],
         cost_estimate=pl.CostEstimate(flops=0, bytes_accessed=4_000_000, transcendentals=0),
         name="reply",
-    )(wanted, points)
+    )(asked, points)
 
 
 def split3(value):
@@ -209,13 +268,18 @@
     return left, right
 
 
-def pair_kernel(first, number, phases, places, *refs):
+def pair_kernel(first, steps, phases, places, *refs):
     replies = refs[:phases]
-    sketch_ref = refs[phases]
-    range_ref, co_ref, turned_ref, left_ref, right_ref = refs[-5:]
+    sketches = refs[phases : phases + 2]
+    range_ref, co_ref = refs[-12:-10]
+    turned, ranged = refs[-10:-8], refs[-8:-6]
+    left_ref, right_ref, range_out, co_out = refs[-6:-2]
+    range_sem, co_sem = refs[-2:]
     p = pl.program_id(0)
-
-    def prepare(pair, slot):
+    slot = lax.rem(p, 2)
+    scale = 1.0 / math.sqrt(PTS)
+
+    def prepare(pair, side):
         row_at, col_at = places[1, pair], places[2, pair]
         rows, cols = replies[0][row_at], replies[0][col_at]
         if phases > 1:
@@ -223,47 +287,109 @@
             rows = jnp.where(early, rows, replies[1][row_at])
             cols = jnp.where(early, cols, replies[1][col_at])
         left, right = distance_operands(rows, cols)
-        left_ref[slot] = left
-        right_ref[slot] = right.T
+        left_ref[side] = left
+        right_ref[side] = right.T
+
+    def send_range(step, side):
+        at = lax.rem(step, 2)
+        return pltpu.make_async_copy(
+            range_out.at[at, side],
+            range_ref.at[places[0, first + 2 * step + side]],
+            range_sem.at[at, side],
+        )
+
+    def send_co(step, side):
+        at = lax.rem(step, 2)
+        return pltpu.make_async_copy(
+            co_out.at[at, side],
+            co_ref.at[places[0, first + 2 * step - 1 + side]],
+            co_sem.at[at, side],
+        )
 
     @pl.when(p == 0)
     def _():
-        prepare(first, 0)
-
-    slot = lax.rem(p, 2)
-    limit = places[3, first + p] * BLK
-    test = sketch_ref[0]
-    active = lax.broadcasted_iota(jnp.int32, (1, RK), 1) < limit
-    masked = jnp.where(active, test, jnp.zeros_like(test)).T
-    block = lax.rsqrt(contract(right_ref[slot], left_ref[slot], 1, 0)).astype(bf16)
-    prepare(first + jnp.minimum(p + 1, number - 1), 1 - slot)
-    ranged = contract(masked, block, 1, 0).astype(bf16)
-    range_ref[0] = ranged.T
-    turned_ref[...] = block.T
-    co_ref[0] = (contract(ranged, turned_ref[...], 1, 0) * (1.0 / math.sqrt(PTS))).astype(bf16)
+        for side in range(2):
+            prepare(first + side, side)
+
+    @pl.when(p >= 2)
+    def _():
+        for side in range(2):
+            send_range(p - 2, side).wait()
+        send_co(p - 2, 1).wait()
+
+    @pl.when(p >= 3)
+    def _():
+        send_co(p - 2, 0).wait()
+
+    following = jnp.minimum(p + 1, steps - 1)
+    for side in range(2):
+        other = 1 - side
+        left, right = left_ref[side], right_ref[side]
+        limit = places[3, first + 2 * p + side] * BLK
+        test = sketches[side][0]
+        active = lax.broadcasted_iota(jnp.int32, (1, RK), 1) < limit
+        masked = jnp.where(active, test, jnp.zeros_like(test)).T
+        for start in range(0, PTS, CHUNK):
+            part = slice(start, start + CHUNK)
+            block = lax.rsqrt(contract(right, left[:, part], 1, 0)).astype(bf16)
+            product = contract(ranged[other][...], turned[other][:, part], 1, 0)
+            co_out[slot, side, :, part] = (product * scale).astype(bf16)
+            if start == 0:
+                prepare(first + 2 * following + side, side)
+            some = contract(masked, block, 1, 0).astype(bf16)
+            range_out[slot, side, part, :] = some.T
+            ranged[side][:, part] = some
+            turned[side][part, :] = block.T
+
+    for side in range(2):
+        send_range(p, side).start()
+    send_co(p, 1).start()
+
+    @pl.when(p >= 1)
+    def _():
+        send_co(p, 0).start()
+
+    @pl.when(p == steps - 1)
+    def _():
+        send_co(p - 1, 0).wait()
+        product = contract(ranged[1][...], turned[1][...], 1, 0)
+        co_out[1 - slot, 0] = (product * scale).astype(bf16)
+        send_co(p + 1, 0).start()
+        for side in range(2):
+            send_range(p - 1, side).wait()
+            send_range(p, side).wait()
+            send_co(p, side).wait()
+        send_co(p - 1, 1).wait()
+        send_co(p + 1, 0).wait()
 
 
 def pair_products(first, number, places, replies, sketch, old):
     count = sketch.shape[0]
-
-    def own(p, places):
-        return (places[0, first + p], 0, 0)
-
-    pair_specs = [pl.BlockSpec((1, PTS, RK), own), pl.BlockSpec((1, RK, PTS), own)]
-    operands = [places] + list(replies) + [sketch] + list(old)
+    steps = number // 2
+    assert number == 2 * steps and steps >= 3
+
+    def own(side):
+        return lambda p, places: (places[0, first + 2 * p + side], 0, 0)
+
+    operands = [places] + list(replies) + [sketch, sketch] + list(old)
     return pl.pallas_call(
-        functools.partial(pair_kernel, first, number, len(replies)),
+        functools.partial(pair_kernel, first, steps, len(replies)),
         grid_spec=pltpu.PrefetchScalarGridSpec(
             num_scalar_prefetch=1,
-            grid=(number,),
+            grid=(steps,),
             in_specs=[pl.BlockSpec(memory_space=pltpu.VMEM) for _ in replies]
-            + pair_specs[:1]
+            + [pl.BlockSpec((1, PTS, RK), own(side)) for side in range(2)]
             + [pl.BlockSpec(memory_space=pl.ANY) for _ in old],
-            out_specs=pair_specs,
-            scratch_shapes=[
-                pltpu.VMEM((PTS, PTS), bf16),
+            out_specs=[pl.BlockSpec(memory_space=pl.ANY)] * 2,
+            scratch_shapes=[pltpu.VMEM((PTS, PTS), bf16)] * 2
+            + [pltpu.VMEM((RK, PTS), bf16)] * 2
+            + [
                 pltpu.VMEM((2, 32, PTS), bf16),
                 pltpu.VMEM((2, PTS, 32), bf16),
+                pltpu.VMEM((2, 2, PTS, RK), bf16),
+                pltpu.VMEM((2, 2, RK, PTS), bf16),
+                pltpu.SemaphoreType.DMA((2, 2)),
+                pltpu.SemaphoreType.DMA((2, 2)),
             ],
         ),
         out_shape=[
@@ -292,10 +418,9 @@
         members,
     )
     asked = lax.all_to_all(wanted, "dev", split_axis=0, concat_axis=0, tiled=True)
-    points = pick(panel_order, panel_coords, panel_weights.reshape(128, 128))
+    points, found = pick(asked, panel_order, panel_coords, panel_weights.reshape(128, 128))
     replies = []
-    for phase in range(2):
-        found = reply(phase, asked, points)
+    for found in (found, reply(asked, points)):
         got = lax.all_to_all(found, "dev", split_axis=0, concat_axis=0, tiled=True)
         replies.append(got.reshape(members * 2, 4, PTS))
     half = count // 2

time: 108 us -> 104 us (0.963)
  blocking collectives: 0 us -> 15.6 us
  starting transfers between devices: 20 us -> 8.04 us
  local copies, waits for them, and re-layouts: 3.93 us -> 0.01 us
  Pallas kernels: 67.5 us -> 64.4 us
    all_to_all x0 -> x1, blocking collectives: none -> 15.6 us  [shards(): lax.all_to_all(wanted, 'dev', split_axis=0, concat_axis=0, tiled=True)]
    all_to_all x1 -> x0, starting transfers between devices: 8.59 us -> none  [shards(): lax.all_to_all(wanted, 'dev', split_axis=0, concat_axis=0, tiled=True)]
    unnamed x12 -> x2, local copies, waits for them, and re-layouts: 3.93 us -> 0.01 us
    all_to_all x2, starting transfers between devices: 11.4 us -> 8.04 us  [shards(): got = lax.all_to_all(found, 'dev', split_axis=0, concat_axis=0, tiled=True)]
    pallas_call x5 -> x4, Pallas kernels: 65.2 us -> 62.1 us  [the longest x2 48.2 us: pair_products(): pl.pallas_call(functools.partial(pair_kernel, first, steps, len(replies))...]
  transfers between devices with their start and end apart: 3 -> 2, of which waited for: 1 -> 1; matrix products, arithmetic and copies ran while one was open for 0% -> 0% of each run, Pallas kernels for 34% -> 26%
where the time goes in v4:
time: 104 us; the launch traced here: 103 us
  Pallas kernels  64.4 us (62%)
  blocking collectives  15.6 us (15%)
  waiting for transfers between devices  14.5 us (14%)
  starting transfers between devices  8.04 us (8%)
    pallas_call x2, Pallas kernels, pair_products(): pl.pallas_call(functools.partial(pair_kernel, first, steps, len(replies))...  48.2 us
    all_to_all x1, blocking collectives, shards(): lax.all_to_all(wanted, 'dev', split_axis=0, concat_axis=0, tiled=True)  15.6 us
    all_to_all x2, waiting for transfers between devices, shards(): got = lax.all_to_all(found, 'dev', split_axis=0, concat_axis=0, tiled=True)  14.5 us
    pallas_call x1, Pallas kernels, pick(): pl.pallas_call(pick_kernel, out_shape=[jax.ShapeDtypeStruct((CL_DEV, 4, P...  11.1 us
    all_to_all x2, starting transfers between devices, shards(): got = lax.all_to_all(found, 'dev', split_axis=0, concat_axis=0, tiled=True)  8.04 us
    pallas_call x1, Pallas kernels, reply(): pl.pallas_call(reply_kernel, in_specs=[pl.BlockSpec(memory_space=pltpu.VM...  2.76 us
    pallas_call x1, Pallas kernels, plan(): pl.pallas_call(plan_kernel, out_shape=[jax.ShapeDtypeStruct((members, 128...  2.33 us
  transfers between devices with their start and end apart: 2, of which 1 were waited for; matrix products, arithmetic and copies ran while one was open for 0% of the time, Pallas kernels for 26%

profile of v4, /device:TPU:1, one launch (start us, length us, event | category | flops | bytes accessed | tf_op | source)
XLA Modules:
  0.0 103.3 jit_solution(10946993467846505032)
XLA Ops:
  0.6 2.3 %plan.1 = (s32[32,128]{1,0:T(8,128)}, s32[8,32]{1,0:T(8,128)}) custom-call(s32[1,32]{1,0:T(1,128)} %bitcast.18, s32[1,32]{1,0:T(1,128)} %bitcast.19, s32[2,32]{1,0:T(2,128)} %bitcast.17, s32[1,32]{1,0:T(1,128)} %bitcast.20), custom_call_target="tpu_custom_call" | custom-call | tf_op jit(solution)/shard_map/plan/pallas_call | solution.py:211
  3.0 15.6 %all_to_all.21 = s32[32,1,128]{2,1,0:T(1,128)} all-to-all(s32[32,1,128]{2,1,0:T(1,128)} %bitcast.16), channel_id=1, replica_groups=mesh['leaf'=4,'dev'=32] {'dev'}, dimensions={0} | all-to-all | bytes 32768 | tf_op jit(solution)/shard_map/all_to_all | solution.py:420
  18.6 0.0 copy-start
  18.6 11.1 %pick.1 = (f32[16,4,1024]{2,1,0:T(4,128)}, f32[32,2,4,1024]{3,2,1,0:T(4,128)}) custom-call(s32[32,128]{1,0:T(8,128)} %bitcast.14, s32[1,16384]{1,0:T(1,128)} %order_hbm.1, f32[3,16384]{1,0:T(4,128)} %coords_hbm.1, f32[128,128]{1,0:T(8,128)} %bitcast.21), custom_call_target="tpu_custom_call" | custom-call | flops 5000000000 | bytes 4000000 | tf_op jit(solution)/shard_map/pick/pallas_call | solution.py:113
  29.6 4.1 %all-to-all-start.1 = ((f32[32,2,4,1024]{3,2,1,0:T(4,128)}), f32[32,2,4,1024]{3,2,1,0:T(4,128)S(1)}, u32[]{:S(2)}, u32[]{:S(2)}) async-start(f32[32,2,4,1024]{3,2,1,0:T(4,128)} %get-tuple-element.10), calls=%async_computation.1 | async-start | bytes 2097152 | tf_op jit(solution)/shard_map/all_to_all | solution.py:424
  33.7 2.8 %reply.1 = f32[32,2,4,1024]{3,2,1,0:T(4,128)} custom-call(s32[32,128]{1,0:T(8,128)} %bitcast.15, f32[16,4,1024]{2,1,0:T(4,128)} %get-tuple-element.11.points_ref), custom_call_target="tpu_custom_call" | custom-call | bytes 4000000 | tf_op jit(solution)/shard_map/reply/pallas_call | solution.py:231
  36.5 14.5 %all-to-all-done.1 = f32[32,2,4,1024]{3,2,1,0:T(4,128)S(1)} async-done(((f32[32,2,4,1024]{3,2,1,0:T(4,128)}), f32[32,2,4,1024]{3,2,1,0:T(4,128)S(1)}, u32[]{:S(2)}, u32[]{:S(2)}) %all-to-all-start.1) | async-done | bytes 1048608 | tf_op jit(solution)/shard_map/all_to_all | solution.py:424
  51.0 4.0 %all-to-all-start.2 = ((f32[32,2,4,1024]{3,2,1,0:T(4,128)}), f32[32,2,4,1024]{3,2,1,0:T(4,128)S(1)}, u32[]{:S(2)}, u32[]{:S(2)}) async-start(f32[32,2,4,1024]{3,2,1,0:T(4,128)} %reply.1), calls=%async_computation.2 | async-start | bytes 2097152 | tf_op jit(solution)/shard_map/all_to_all | solution.py:424
  55.0 0.0 copy-done
  55.0 24.1 %pairs.2 = (bf16[32,1024,128]{2,1,0:T(8,128)(2,1)}, bf16[32,128,1024]{2,1,0:T(8,128)(2,1)}) custom-call(s32[8,32]{1,0:T(8,128)S(1)} %copy-done, f32[64,4,1024]{2,1,0:T(4,128)S(1)} %bitcast.11, bf16[32,1024,128]{2,1,0:T(8,128)(2,1)} %refs_3_.1, bf16[32,1024,128]{2,1,0:T(8,128)(2,1)} %refs_3_.1), custom_call_target="tpu_custom_call" | custom-call | flops 25769803776 | bytes 12800000 | tf_op jit(solution)/shard_map/pairs/pallas_call | solution.py:375
  79.1 0.0 all-to-all-done.2
  79.1 24.1 %pairs.3 = (bf16[32,1024,128]{2,1,0:T(8,128)(2,1)}, bf16[32,128,1024]{2,1,0:T(8,128)(2,1)}) custom-call(s32[8,32]{1,0:T(8,128)S(1)} %copy-done, f32[64,4,1024]{2,1,0:T(4,128)S(1)} %bitcast.12, f32[64,4,1024]{2,1,0:T(4,128)S(1)} %bitcast.13, bf16[32,1024,128]{2,1,0:T(8,128)(2,1)} %refs_3_.1, ...), custom_call_target="tpu_custom_call", output_to_operand_aliasing={{0}: (5, {}), {1}: (6, {})} | custom-call | flops 25769803776 | bytes 12800000 | tf_op jit(solution)/shard_map/pairs/pallas_call | solution.py:375
Async XLA Ops:
  18.6 36.4 %copy-start = (s32[8,32]{1,0:T(8,128)S(1)}, s32[8,32]{1,0:T(8,128)}, u32[]{:S(2)}) copy-start(s32[8,32]{1,0:T(8,128)} %get-tuple-element.8.places) | copy-start | bytes 3076
  29.6 21.4 %all-to-all-start.1 = ((f32[32,2,4,1024]{3,2,1,0:T(4,128)}), f32[32,2,4,1024]{3,2,1,0:T(4,128)S(1)}, u32[]{:S(2)}, u32[]{:S(2)}) async-start(f32[32,2,4,1024]{3,2,1,0:T(4,128)} %get-tuple-element.10), calls=%async_computation.1 | async-start | bytes 2097152 | tf_op jit(solution)/shard_map/all_to_all | solution.py:424
  51.0 28.1 %all-to-all-start.2 = ((f32[32,2,4,1024]{3,2,1,0:T(4,128)}), f32[32,2,4,1024]{3,2,1,0:T(4,128)S(1)}, u32[]{:S(2)}, u32[]{:S(2)}) async-start(f32[32,2,4,1024]{3,2,1,0:T(4,128)} %reply.1), calls=%async_computation.2 | async-start | bytes 2097152 | tf_op jit(solution)/shard_map/all_to_all | solution.py:424

commit v5 on v4

--- a/solution.py
+++ b/solution.py
@@ -26,42 +26,12 @@
 LANES = 256
 
 
-def pick_kernel(
-    asked_ref,
-    order_hbm,
-    coords_hbm,
-    weights_hbm,
-    out_ref,
-    found_ref,
-    order_ref,
-    coords_ref,
-    weights_ref,
-    asked_smem,
-    table_ref,
-    split_ref,
-    sems,
-    found_sem,
-):
-    fetches = [
-        pltpu.make_async_copy(source, target, sems.at[i])
-        for i, (source, target) in enumerate(
-            (
-                (coords_hbm, coords_ref),
-                (weights_hbm, weights_ref),
-                (order_hbm, order_ref),
-                (asked_ref, asked_smem),
-            )
-        )
-    ]
-    for fetch in fetches:
-        fetch.start()
-    fetches[0].wait()
+def pick_kernel(order_ref, coords_ref, weights_ref, out_ref, table_ref, split_ref):
     for part in range(3):
         for m in range(64):
             table_ref[part * 64 + m : part * 64 + m + 1, :] = coords_ref[
                 part : part + 1, m * 256 : m * 256 + 256
             ]
-    fetches[1].wait()
     for half in range(2):
         table_ref[192:256, half * 128 : half * 128 + 128] = weights_ref[
             pl.ds(half, 64, stride=2), :
@@ -71,12 +41,11 @@
     split_ref[:, 0:256] = head
     split_ref[:, 256:512] = (table - head.astype(f32)).astype(bf16)
 
-    fetches[2].wait()
-
     def some_points(cluster, lane):
         index = order_ref[0:1, pl.ds(pl.multiple_of(cluster * PTS + lane, LANES), LANES)]
-        k = lax.broadcasted_iota(jnp.int32, (256, LANES), 0)
-        hot = jnp.where(k == (index & 255), 1.0, 0.0).astype(bf16)
+        k = lax.broadcasted_iota(jnp.int32, (256, LANES), 0).astype(f32).astype(bf16)
+        low = (index & 255).astype(f32).astype(bf16)
+        hot = jnp.where(k == low, jnp.ones((), bf16), jnp.zeros((), bf16))
         found = contract(split_ref[...], jnp.concatenate([hot, hot], axis=0), 1, 0)
         m = lax.broadcasted_iota(jnp.int32, (64, LANES), 0)
         here = m == (index >> 8)
@@ -93,51 +62,21 @@
         return carry
 
     lax.fori_loop(0, CL_DEV // PICK_TURN, turn, 0)
-    fetches[3].wait()
-    send_found(0, asked_smem, out_ref, found_ref, found_sem)
-
-
-def send_found(phase, asked_smem, points_ref, found_ref, sem):
-    for member in range(found_ref.shape[0]):
-        for side in range(2):
-            pltpu.make_async_copy(
-                points_ref.at[asked_smem[member, phase * 2 + side]],
-                found_ref.at[member, side],
-                sem,
-            ).start()
-    pltpu.make_async_copy(found_ref, found_ref, sem).wait()
-
-
-def pick(asked, order, coords, weights):
-    members = asked.shape[0]
+
+
+def pick(order, coords, weights):
     return pl.pallas_call(
         pick_kernel,
-        out_shape=[
-            jax.ShapeDtypeStruct((CL_DEV, 4, PTS), f32),
-            jax.ShapeDtypeStruct((members, 2, 4, PTS), f32),
-        ],
-        in_specs=[pl.BlockSpec(memory_space=pltpu.VMEM)]
-        + [pl.BlockSpec(memory_space=pltpu.HBM)] * 3,
-        out_specs=[
-            pl.BlockSpec(memory_space=pltpu.VMEM),
-            pl.BlockSpec(memory_space=pltpu.HBM),
-        ],
-        scratch_shapes=[
-            pltpu.VMEM(order.shape, jnp.int32),
-            pltpu.VMEM(coords.shape, f32),
-            pltpu.VMEM(weights.shape, f32),
-            pltpu.SMEM(asked.shape, jnp.int32),
-            pltpu.VMEM((256, 256), f32),
-            pltpu.VMEM((256, 512), bf16),
-            pltpu.SemaphoreType.DMA((4,)),
-            pltpu.SemaphoreType.DMA,
-        ],
-        compiler_params=pltpu.CompilerParams(vmem_limit_bytes=56 << 20),
+        out_shape=jax.ShapeDtypeStruct((CL_DEV, 4, PTS), f32),
+        in_specs=[pl.BlockSpec(memory_space=pltpu.VMEM)] * 3,
+        out_specs=pl.BlockSpec(memory_space=pltpu.VMEM),
+        scratch_shapes=[pltpu.VMEM((256, 256), f32), pltpu.VMEM((256, 512), bf16)],
+        compiler_params=pltpu.CompilerParams(vmem_limit_bytes=32 << 20),
         cost_estimate=pl.CostEstimate(
-            flops=5_000_000_000, bytes_accessed=4_000_000, transcendentals=0
+            flops=5_000_000_000, bytes_accessed=600_000, transcendentals=0
         ),
         name="pick",
-    )(asked, order, coords, weights)
+    )(order, coords, weights)
 
 
 def plan_kernel(row_ref, col_ref, slots_ref, rank_ref, wanted_ref, places_ref):
@@ -220,17 +159,24 @@
     )(row_owner, col_owner, slots, rank)
 
 
-def reply_kernel(asked_ref, points_ref, found_ref, asked_smem, asked_sem, sem):
+def reply_kernel(phase, asked_ref, points_ref, found_ref, asked_smem, asked_sem, sem):
     fetch = pltpu.make_async_copy(asked_ref, asked_smem, asked_sem)
     fetch.start()
     fetch.wait()
-    send_found(1, asked_smem, points_ref, found_ref, sem)
-
-
-def reply(asked, points):
+    for member in range(found_ref.shape[0]):
+        for side in range(2):
+            pltpu.make_async_copy(
+                points_ref.at[asked_smem[member, phase * 2 + side]],
+                found_ref.at[member, side],
+                sem,
+            ).start()
+    pltpu.make_async_copy(found_ref, found_ref, sem).wait()
+
+
+def reply(phase, asked, points):
     return pl.pallas_call(
-        reply_kernel,
-        in_specs=[pl.BlockSpec(memory_space=pltpu.VMEM)] * 2,
+        functools.partial(reply_kernel, phase),
+        in_specs=[pl.BlockSpec(memory_space=pl.ANY), pl.BlockSpec(memory_space=pltpu.VMEM)],
         out_specs=pl.BlockSpec(memory_space=pltpu.HBM),
         out_shape=jax.ShapeDtypeStruct((asked.shape[0], 2, 4, PTS), f32),
         scratch_shapes=[
@@ -418,9 +364,10 @@
         members,
     )
     asked = lax.all_to_all(wanted, "dev", split_axis=0, concat_axis=0, tiled=True)
-    points, found = pick(asked, panel_order, panel_coords, panel_weights.reshape(128, 128))
+    points = pick(panel_order, panel_coords, panel_weights.reshape(128, 128))
     replies = []
-    for found in (found, reply(asked, points)):
+    for phase in range(2):
+        found = reply(phase, asked, points)
         got = lax.all_to_all(found, "dev", split_axis=0, concat_axis=0, tiled=True)
         replies.append(got.reshape(members * 2, 4, PTS))
     half = count // 2

time: 104 us -> 102 us (0.981)
  blocking collectives: 15.6 us -> 0 us
  starting transfers between devices: 8.04 us -> 20 us
  local copies, waits for them, and re-layouts: 0.01 us -> 3.93 us
  Pallas kernels: 64.4 us -> 62.4 us
    all_to_all x1 -> x0, blocking collectives: 15.6 us -> none  [shards(): lax.all_to_all(wanted, 'dev', split_axis=0, concat_axis=0, tiled=True)]
    all_to_all x0 -> x1, starting transfers between devices: none -> 8.59 us  [shards(): lax.all_to_all(wanted, 'dev', split_axis=0, concat_axis=0, tiled=True)]
    unnamed x2 -> x12, local copies, waits for them, and re-layouts: 0.01 us -> 3.93 us
    all_to_all x2, starting transfers between devices: 8.04 us -> 11.4 us  [shards(): got = lax.all_to_all(found, 'dev', split_axis=0, concat_axis=0, tiled=True)]
    pallas_call x2 -> x3, Pallas kernels: 13.8 us -> 11.8 us  [the longest x1 6.14 us: pick(): pl.pallas_call(pick_kernel, out_shape=jax.ShapeDtypeStruct((CL_DEV, 4, PT...]
  transfers between devices with their start and end apart: 2 -> 3, of which waited for: 1 -> 1; matrix products, arithmetic and copies ran while one was open for 0% -> 0% of each run, Pallas kernels for 26% -> 33%
where the time goes in v5:
time: 102 us; the launch traced here: 101 us
  Pallas kernels  62.4 us (61%)
  starting transfers between devices  20 us (20%)
  waiting for transfers between devices  14.3 us (14%)
  local copies, waits for them, and re-layouts  3.93 us (4%)
    pallas_call x2, Pallas kernels, pair_products(): pl.pallas_call(functools.partial(pair_kernel, first, steps, len(replies))...  48.2 us
    all_to_all x2, waiting for transfers between devices, shards(): got = lax.all_to_all(found, 'dev', split_axis=0, concat_axis=0, tiled=True)  14.3 us
    all_to_all x2, starting transfers between devices, shards(): got = lax.all_to_all(found, 'dev', split_axis=0, concat_axis=0, tiled=True)  11.4 us
    all_to_all x1, starting transfers between devices, shards(): lax.all_to_all(wanted, 'dev', split_axis=0, concat_axis=0, tiled=True)  8.59 us
    pallas_call x1, Pallas kernels, pick(): pl.pallas_call(pick_kernel, out_shape=jax.ShapeDtypeStruct((CL_DEV, 4, PT...  6.14 us
    pallas_call x2, Pallas kernels, reply(): pl.pallas_call(functools.partial(reply_kernel, phase), in_specs=[pl.Block...  5.69 us
    unnamed x12, local copies, waits for them, and re-layouts  3.93 us
    pallas_call x1, Pallas kernels, plan(): pl.pallas_call(plan_kernel, out_shape=[jax.ShapeDtypeStruct((members, 128...  2.33 us
  transfers between devices with their start and end apart: 3, of which 1 were waited for; matrix products, arithmetic and copies ran while one was open for 0% of the time, Pallas kernels for 33%

profile of v5, /device:TPU:1, one launch (start us, length us, event | category | flops | bytes accessed | tf_op | source)
XLA Modules:
  0.0 101.3 jit_solution(11250266648864305755)
XLA Ops:
  0.6 2.3 %plan.1 = (s32[32,128]{1,0:T(8,128)}, s32[8,32]{1,0:T(8,128)}) custom-call(s32[1,32]{1,0:T(1,128)} %bitcast.19, s32[1,32]{1,0:T(1,128)} %bitcast.20, s32[2,32]{1,0:T(2,128)} %bitcast.18, s32[1,32]{1,0:T(1,128)} %bitcast.21), custom_call_target="tpu_custom_call" | custom-call | tf_op jit(solution)/shard_map/plan/pallas_call | solution.py:150
  3.0 8.6 %all-to-all-start = ((s32[32,1,128]{2,1,0:T(1,128)}), s32[32,1,128]{2,1,0:T(1,128)S(1)}, u32[]{:S(2)}, u32[]{:S(2)}) async-start(s32[32,1,128]{2,1,0:T(1,128)} %bitcast.17), calls=%async_computation | async-start | bytes 32768 | tf_op jit(solution)/shard_map/all_to_all | solution.py:366
  11.6 0.0 copy-start.1
  11.6 0.9 copy-done.1
  12.5 0.0 copy-start.2
  12.5 0.8 copy-done.2
  13.4 0.0 copy-start.3
  13.4 0.8 copy-done.3
  14.2 0.0 copy-start.4
  14.2 6.1 %pick.1.points_ref = f32[16,4,1024]{2,1,0:T(4,128)S(1)} custom-call(s32[1,16384]{1,0:T(1,128)S(1)} %copy-done.2, f32[3,16384]{1,0:T(4,128)S(1)} %copy-done.1, f32[128,128]{1,0:T(8,128)S(1)} %bitcast.14), custom_call_target="tpu_custom_call" | custom-call | flops 5000000000 | bytes 600000 | tf_op jit(solution)/shard_map/pick/pallas_call | solution.py:68
  20.3 0.0 copy-start
  20.4 0.7 copy-done
  21.0 0.0 all-to-all-done
  21.0 0.0 copy-start.5
  21.1 0.6 copy-done.5
  21.7 2.8 %reply.2 = f32[32,2,4,1024]{3,2,1,0:T(4,128)} custom-call(s32[32,128]{1,0:T(8,128)} %bitcast.15, f32[16,4,1024]{2,1,0:T(4,128)} %copy-done), custom_call_target="tpu_custom_call" | custom-call | bytes 4000000 | tf_op jit(solution)/shard_map/reply/pallas_call | solution.py:177
  24.5 7.4 %all-to-all-start.1 = ((f32[32,2,4,1024]{3,2,1,0:T(4,128)}), f32[32,2,4,1024]{3,2,1,0:T(4,128)S(1)}, u32[]{:S(2)}, u32[]{:S(2)}) async-start(f32[32,2,4,1024]{3,2,1,0:T(4,128)} %reply.2), calls=%async_computation.1 | async-start | bytes 2097152 | tf_op jit(solution)/shard_map/all_to_all | solution.py:371
  31.9 2.9 %reply.3 = f32[32,2,4,1024]{3,2,1,0:T(4,128)} custom-call(s32[32,128]{1,0:T(8,128)} %bitcast.16, f32[16,4,1024]{2,1,0:T(4,128)} %copy-done), custom_call_target="tpu_custom_call" | custom-call | bytes 4000000 | tf_op jit(solution)/shard_map/reply/pallas_call | solution.py:177
  34.8 14.3 %all-to-all-done.1 = f32[32,2,4,1024]{3,2,1,0:T(4,128)S(1)} async-done(((f32[32,2,4,1024]{3,2,1,0:T(4,128)}), f32[32,2,4,1024]{3,2,1,0:T(4,128)S(1)}, u32[]{:S(2)}, u32[]{:S(2)}) %all-to-all-start.1) | async-done | bytes 1048608 | tf_op jit(solution)/shard_map/all_to_all | solution.py:371
  49.1 4.0 %all-to-all-start.2 = ((f32[32,2,4,1024]{3,2,1,0:T(4,128)}), f32[32,2,4,1024]{3,2,1,0:T(4,128)S(1)}, u32[]{:S(2)}, u32[]{:S(2)}) async-start(f32[32,2,4,1024]{3,2,1,0:T(4,128)} %reply.3), calls=%async_computation.2 | async-start | bytes 2097152 | tf_op jit(solution)/shard_map/all_to_all | solution.py:371
  53.1 0.0 copy-done.4
  53.1 24.1 %pairs.2 = (bf16[32,1024,128]{2,1,0:T(8,128)(2,1)}, bf16[32,128,1024]{2,1,0:T(8,128)(2,1)}) custom-call(s32[8,32]{1,0:T(8,128)S(1)} %copy-done.4, f32[64,4,1024]{2,1,0:T(4,128)S(1)} %bitcast.11, bf16[32,1024,128]{2,1,0:T(8,128)(2,1)} %refs_3_.1, bf16[32,1024,128]{2,1,0:T(8,128)(2,1)} %refs_3_.1), custom_call_target="tpu_custom_call" | custom-call | flops 25769803776 | bytes 12800000 | tf_op jit(solution)/shard_map/pairs/pallas_call | solution.py:321
  77.2 0.0 all-to-all-done.2
  77.2 24.1 %pairs.3 = (bf16[32,1024,128]{2,1,0:T(8,128)(2,1)}, bf16[32,128,1024]{2,1,0:T(8,128)(2,1)}) custom-call(s32[8,32]{1,0:T(8,128)S(1)} %copy-done.4, f32[64,4,1024]{2,1,0:T(4,128)S(1)} %bitcast.12, f32[64,4,1024]{2,1,0:T(4,128)S(1)} %bitcast.13, bf16[32,1024,128]{2,1,0:T(8,128)(2,1)} %refs_3_.1, ...), custom_call_target="tpu_custom_call", output_to_operand_aliasing={{0}: (5, {}), {1}: (6, {})} | custom-call | flops 25769803776 | bytes 12800000 | tf_op jit(solution)/shard_map/pairs/pallas_call | solution.py:321
Async XLA Ops:
  3.0 18.1 %all-to-all-start = ((s32[32,1,128]{2,1,0:T(1,128)}), s32[32,1,128]{2,1,0:T(1,128)S(1)}, u32[]{:S(2)}, u32[]{:S(2)}) async-start(s32[32,1,128]{2,1,0:T(1,128)} %bitcast.17), calls=%async_computation | async-start | bytes 32768 | tf_op jit(solution)/shard_map/all_to_all | solution.py:366
  11.6 1.0 copy-start.1
  12.5 0.8 copy-start.2
  13.4 0.8 copy-start.3
  14.2 38.9 %copy-start.4 = (s32[8,32]{1,0:T(8,128)S(1)}, s32[8,32]{1,0:T(8,128)}, u32[]{:S(2)}) copy-start(s32[8,32]{1,0:T(8,128)} %get-tuple-element.6.places) | copy-start | bytes 3076
  20.3 0.7 copy-start
  21.0 0.6 copy-start.5
  24.5 24.6 %all-to-all-start.1 = ((f32[32,2,4,1024]{3,2,1,0:T(4,128)}), f32[32,2,4,1024]{3,2,1,0:T(4,128)S(1)}, u32[]{:S(2)}, u32[]{:S(2)}) async-start(f32[32,2,4,1024]{3,2,1,0:T(4,128)} %reply.2), calls=%async_computation.1 | async-start | bytes 2097152 | tf_op jit(solution)/shard_map/all_to_all | solution.py:371
  49.1 28.1 %all-to-all-start.2 = ((f32[32,2,4,1024]{3,2,1,0:T(4,128)}), f32[32,2,4,1024]{3,2,1,0:T(4,128)S(1)}, u32[]{:S(2)}, u32[]{:S(2)}) async-start(f32[32,2,4,1024]{3,2,1,0:T(4,128)} %reply.3), calls=%async_computation.2 | async-start | bytes 2097152 | tf_op jit(solution)/shard_map/all_to_all | solution.py:371

commit v6 on v5

--- a/solution.py
+++ b/solution.py
@@ -22,7 +22,7 @@
 def contract(a, b, dim_a, dim_b):
     return lax.dot_general(a, b, (((dim_a,), (dim_b,)), ((), ())), preferred_element_type=f32)
 
-PICK_TURN = 2
+PICK_TURN = 8
 LANES = 256
 
 
@@ -184,6 +184,7 @@
             pltpu.SemaphoreType.DMA,
             pltpu.SemaphoreType.DMA,
         ],
+        compiler_params=pltpu.CompilerParams(vmem_limit_bytes=4 << 20),
         cost_estimate=pl.CostEstimate(flops=0, bytes_accessed=4_000_000, transcendentals=0),
         name="reply",
     )(asked, points)

time: 102 us -> 98.4 us (0.965)
  Pallas kernels: 62.4 us -> 59.1 us
  local copies, waits for them, and re-layouts: 3.93 us -> 2.63 us
  waiting for transfers between devices: 14.3 us -> 15.4 us
    pallas_call x2, Pallas kernels: 5.69 us -> 3.55 us  [reply(): pl.pallas_call(functools.partial(reply_kernel, phase), in_specs=[pl.Block...]
    unnamed x12 -> x8, local copies, waits for them, and re-layouts: 3.93 us -> 2.63 us
    pallas_call x1, Pallas kernels: 6.14 us -> 5.01 us  [pick(): pl.pallas_call(pick_kernel, out_shape=jax.ShapeDtypeStruct((CL_DEV, 4, PT...]
    all_to_all x2, waiting for transfers between devices: 14.3 us -> 15.4 us  [shards(): got = lax.all_to_all(found, 'dev', split_axis=0, concat_axis=0, tiled=True)]
  transfers between devices with their start and end apart: 3 -> 3, of which waited for: 1 -> 1; matrix products, arithmetic and copies ran while one was open for 0% -> 0% of each run, Pallas kernels for 33% -> 32%
where the time goes in v6:
time: 98.4 us; the launch traced here: 97.8 us
  Pallas kernels  59.1 us (60%)
  starting transfers between devices  20 us (20%)
  waiting for transfers between devices  15.4 us (16%)
  local copies, waits for them, and re-layouts  2.63 us (3%)
    pallas_call x2, Pallas kernels, pair_products(): pl.pallas_call(functools.partial(pair_kernel, first, steps, len(replies))...  48.2 us
    all_to_all x2, waiting for transfers between devices, shards(): got = lax.all_to_all(found, 'dev', split_axis=0, concat_axis=0, tiled=True)  15.4 us
    all_to_all x2, starting transfers between devices, shards(): got = lax.all_to_all(found, 'dev', split_axis=0, concat_axis=0, tiled=True)  11.4 us
    all_to_all x1, starting transfers between devices, shards(): lax.all_to_all(wanted, 'dev', split_axis=0, concat_axis=0, tiled=True)  8.59 us
    pallas_call x1, Pallas kernels, pick(): pl.pallas_call(pick_kernel, out_shape=jax.ShapeDtypeStruct((CL_DEV, 4, PT...  5.01 us
    pallas_call x2, Pallas kernels, reply(): pl.pallas_call(functools.partial(reply_kernel, phase), in_specs=[pl.Block...  3.55 us
    unnamed x8, local copies, waits for them, and re-layouts  2.63 us
    pallas_call x1, Pallas kernels, plan(): pl.pallas_call(plan_kernel, out_shape=[jax.ShapeDtypeStruct((members, 128...  2.33 us
  transfers between devices with their start and end apart: 3, of which 1 were waited for; matrix products, arithmetic and copies ran while one was open for 0% of the time, Pallas kernels for 32%

profile of v6, /device:TPU:1, one launch (start us, length us, event | category | flops | bytes accessed | tf_op | source)
XLA Modules:
  0.0 97.8 jit_solution(1649698181068247435)
XLA Ops:
  0.6 2.3 %plan.1 = (s32[32,128]{1,0:T(8,128)}, s32[8,32]{1,0:T(8,128)}) custom-call(s32[1,32]{1,0:T(1,128)} %bitcast.19, s32[1,32]{1,0:T(1,128)} %bitcast.20, s32[2,32]{1,0:T(2,128)} %bitcast.18, s32[1,32]{1,0:T(1,128)} %bitcast.21), custom_call_target="tpu_custom_call" | custom-call | tf_op jit(solution)/shard_map/plan/pallas_call | solution.py:150
  3.0 8.6 %all-to-all-start = ((s32[32,1,128]{2,1,0:T(1,128)}), s32[32,1,128]{2,1,0:T(1,128)S(1)}, u32[]{:S(2)}, u32[]{:S(2)}) async-start(s32[32,1,128]{2,1,0:T(1,128)} %bitcast.17), calls=%async_computation | async-start | bytes 32768 | tf_op jit(solution)/shard_map/all_to_all | solution.py:367
  11.6 0.0 copy-start
  11.6 0.9 copy-done
  12.5 0.0 copy-start.1
  12.5 0.8 copy-done.1
  13.4 0.0 copy-start.2
  13.4 0.8 copy-done.2
  14.2 0.0 copy-start.3
  14.2 5.0 %pick.1.points_ref = f32[16,4,1024]{2,1,0:T(4,128)S(1)} custom-call(s32[1,16384]{1,0:T(1,128)S(1)} %copy-done.1, f32[3,16384]{1,0:T(4,128)S(1)} %copy-done, f32[128,128]{1,0:T(8,128)S(1)} %bitcast.16), custom_call_target="tpu_custom_call" | custom-call | flops 5000000000 | bytes 600000 | tf_op jit(solution)/shard_map/pick/pallas_call | solution.py:68
  19.2 0.0 all-to-all-done
  19.2 1.8 %reply.2 = f32[32,2,4,1024]{3,2,1,0:T(4,128)} custom-call(s32[32,128]{1,0:T(8,128)S(1)} %bitcast.14, f32[16,4,1024]{2,1,0:T(4,128)S(1)} %pick.1.points_ref), custom_call_target="tpu_custom_call" | custom-call | bytes 4000000 | tf_op jit(solution)/shard_map/reply/pallas_call | solution.py:177
  21.0 7.4 %all-to-all-start.1 = ((f32[32,2,4,1024]{3,2,1,0:T(4,128)}), f32[32,2,4,1024]{3,2,1,0:T(4,128)S(1)}, u32[]{:S(2)}, u32[]{:S(2)}) async-start(f32[32,2,4,1024]{3,2,1,0:T(4,128)} %reply.2), calls=%async_computation.1 | async-start | bytes 2097152 | tf_op jit(solution)/shard_map/all_to_all | solution.py:372
  28.4 1.8 %reply.3 = f32[32,2,4,1024]{3,2,1,0:T(4,128)} custom-call(s32[32,128]{1,0:T(8,128)S(1)} %bitcast.15, f32[16,4,1024]{2,1,0:T(4,128)S(1)} %pick.1.points_ref), custom_call_target="tpu_custom_call" | custom-call | bytes 4000000 | tf_op jit(solution)/shard_map/reply/pallas_call | solution.py:177
  30.2 15.4 %all-to-all-done.1 = f32[32,2,4,1024]{3,2,1,0:T(4,128)S(1)} async-done(((f32[32,2,4,1024]{3,2,1,0:T(4,128)}), f32[32,2,4,1024]{3,2,1,0:T(4,128)S(1)}, u32[]{:S(2)}, u32[]{:S(2)}) %all-to-all-start.1) | async-done | bytes 1048608 | tf_op jit(solution)/shard_map/all_to_all | solution.py:372
  45.6 4.0 %all-to-all-start.2 = ((f32[32,2,4,1024]{3,2,1,0:T(4,128)}), f32[32,2,4,1024]{3,2,1,0:T(4,128)S(1)}, u32[]{:S(2)}, u32[]{:S(2)}) async-start(f32[32,2,4,1024]{3,2,1,0:T(4,128)} %reply.3), calls=%async_computation.2 | async-start | bytes 2097152 | tf_op jit(solution)/shard_map/all_to_all | solution.py:372
  49.6 0.0 copy-done.3
  49.6 24.1 %pairs.2 = (bf16[32,1024,128]{2,1,0:T(8,128)(2,1)}, bf16[32,128,1024]{2,1,0:T(8,128)(2,1)}) custom-call(s32[8,32]{1,0:T(8,128)S(1)} %copy-done.3, f32[64,4,1024]{2,1,0:T(4,128)S(1)} %bitcast.11, bf16[32,1024,128]{2,1,0:T(8,128)(2,1)} %refs_3_.1, bf16[32,1024,128]{2,1,0:T(8,128)(2,1)} %refs_3_.1), custom_call_target="tpu_custom_call" | custom-call | flops 25769803776 | bytes 12800000 | tf_op jit(solution)/shard_map/pairs/pallas_call | solution.py:322
  73.7 0.0 all-to-all-done.2
  73.7 24.1 %pairs.3 = (bf16[32,1024,128]{2,1,0:T(8,128)(2,1)}, bf16[32,128,1024]{2,1,0:T(8,128)(2,1)}) custom-call(s32[8,32]{1,0:T(8,128)S(1)} %copy-done.3, f32[64,4,1024]{2,1,0:T(4,128)S(1)} %bitcast.12, f32[64,4,1024]{2,1,0:T(4,128)S(1)} %bitcast.13, bf16[32,1024,128]{2,1,0:T(8,128)(2,1)} %refs_3_.1, ...), custom_call_target="tpu_custom_call", output_to_operand_aliasing={{0}: (5, {}), {1}: (6, {})} | custom-call | flops 25769803776 | bytes 12800000 | tf_op jit(solution)/shard_map/pairs/pallas_call | solution.py:322
Async XLA Ops:
  3.0 16.3 %all-to-all-start = ((s32[32,1,128]{2,1,0:T(1,128)}), s32[32,1,128]{2,1,0:T(1,128)S(1)}, u32[]{:S(2)}, u32[]{:S(2)}) async-start(s32[32,1,128]{2,1,0:T(1,128)} %bitcast.17), calls=%async_computation | async-start | bytes 32768 | tf_op jit(solution)/shard_map/all_to_all | solution.py:367
  11.6 1.0 copy-start
  12.5 0.8 copy-start.1
  13.4 0.8 copy-start.2
  14.2 35.4 %copy-start.3 = (s32[8,32]{1,0:T(8,128)S(1)}, s32[8,32]{1,0:T(8,128)}, u32[]{:S(2)}) copy-start(s32[8,32]{1,0:T(8,128)} %get-tuple-element.6.places) | copy-start | bytes 3076
  21.0 24.6 %all-to-all-start.1 = ((f32[32,2,4,1024]{3,2,1,0:T(4,128)}), f32[32,2,4,1024]{3,2,1,0:T(4,128)S(1)}, u32[]{:S(2)}, u32[]{:S(2)}) async-start(f32[32,2,4,1024]{3,2,1,0:T(4,128)} %reply.2), calls=%async_computation.1 | async-start | bytes 2097152 | tf_op jit(solution)/shard_map/all_to_all | solution.py:372
  45.6 28.1 %all-to-all-start.2 = ((f32[32,2,4,1024]{3,2,1,0:T(4,128)}), f32[32,2,4,1024]{3,2,1,0:T(4,128)S(1)}, u32[]{:S(2)}, u32[]{:S(2)}) async-start(f32[32,2,4,1024]{3,2,1,0:T(4,128)} %reply.3), calls=%async_computation.2 | async-start | bytes 2097152 | tf_op jit(solution)/shard_map/all_to_all | solution.py:372

commit v7 on v6

--- a/solution.py
+++ b/solution.py
@@ -51,9 +51,10 @@
         here = m == (index >> 8)
         for part in range(4):
             rows = found[part * 64 : part * 64 + 64]
-            out_ref[cluster, part : part + 1, lane : lane + LANES] = jnp.sum(
-                jnp.where(here, rows, 0.0), axis=0, keepdims=True
-            )
+            value = jnp.sum(jnp.where(here, rows, 0.0), axis=0, keepdims=True)
+            for start in range(0, LANES, 128):
+                line = part * 8 + (lane + start) // 128
+                out_ref[cluster, line : line + 1, :] = value[:, start : start + 128]
 
     def turn(number, carry):
         for inner in range(PICK_TURN):
@@ -67,7 +68,7 @@
 def pick(order, coords, weights):
     return pl.pallas_call(
         pick_kernel,
-        out_shape=jax.ShapeDtypeStruct((CL_DEV, 4, PTS), f32),
+        out_shape=jax.ShapeDtypeStruct((CL_DEV, 32, 128), f32),
         in_specs=[pl.BlockSpec(memory_space=pltpu.VMEM)] * 3,
         out_specs=pl.BlockSpec(memory_space=pltpu.VMEM),
         scratch_shapes=[pltpu.VMEM((256, 256), f32), pltpu.VMEM((256, 512), bf16)],
@@ -125,8 +126,8 @@
 
     places = [
         ordered(number_down),
-        ordered(column(row_owner * 2.0)),
-        ordered(column(col_owner * 2.0 + 1.0)),
+        ordered(column(row_owner)),
+        ordered(column(col_owner)),
         ordered(column(rank)),
         ordered(1.0 - first),
     ]
@@ -164,10 +165,10 @@
     fetch.start()
     fetch.wait()
     for member in range(found_ref.shape[0]):
-        for side in range(2):
+        for side, (start, size) in enumerate(((0, 24), (24, 32))):
             pltpu.make_async_copy(
-                points_ref.at[asked_smem[member, phase * 2 + side]],
-                found_ref.at[member, side],
+                points_ref.at[asked_smem[member, phase * 2 + side], pl.ds(0, size)],
+                found_ref.at[member, pl.ds(start, size)],
                 sem,
             ).start()
     pltpu.make_async_copy(found_ref, found_ref, sem).wait()
@@ -178,7 +179,7 @@
         functools.partial(reply_kernel, phase),
         in_specs=[pl.BlockSpec(memory_space=pl.ANY), pl.BlockSpec(memory_space=pltpu.VMEM)],
         out_specs=pl.BlockSpec(memory_space=pltpu.HBM),
-        out_shape=jax.ShapeDtypeStruct((asked.shape[0], 2, 4, PTS), f32),
+        out_shape=jax.ShapeDtypeStruct((asked.shape[0], 56, 128), f32),
         scratch_shapes=[
             pltpu.SMEM(asked.shape, jnp.int32),
             pltpu.SemaphoreType.DMA,
@@ -226,13 +227,18 @@
     slot = lax.rem(p, 2)
     scale = 1.0 / math.sqrt(PTS)
 
+    def cluster(reply_ref, at, start):
+        return jnp.concatenate(
+            [reply_ref[at, pl.ds(start + line, 4, stride=8), :] for line in range(8)], axis=1
+        )
+
     def prepare(pair, side):
         row_at, col_at = places[1, pair], places[2, pair]
-        rows, cols = replies[0][row_at], replies[0][col_at]
+        rows, cols = cluster(replies[0], row_at, 0), cluster(replies[0], col_at, 24)
         if phases > 1:
             early = places[4, pair] == 0
-            rows = jnp.where(early, rows, replies[1][row_at])
-            cols = jnp.where(early, cols, replies[1][col_at])
+            rows = jnp.where(early, rows, cluster(replies[1], row_at, 0))
+            cols = jnp.where(early, cols, cluster(replies[1], col_at, 24))
         left, right = distance_operands(rows, cols)
         left_ref[side] = left
         right_ref[side] = right.T
@@ -370,7 +376,7 @@
     for phase in range(2):
         found = reply(phase, asked, points)
         got = lax.all_to_all(found, "dev", split_axis=0, concat_axis=0, tiled=True)
-        replies.append(got.reshape(members * 2, 4, PTS))
+        replies.append(got)
     half = count // 2
     early = pair_products(0, half, places, replies[:1], sketch, ())
     return tuple(pair_products(half, count - half, places, replies, sketch, early))

time: 98.4 us -> 96.9 us (0.985)
  waiting for transfers between devices: 15.4 us -> 14 us
    all_to_all x2, waiting for transfers between devices: 15.4 us -> 14 us  [shards(): got = lax.all_to_all(found, 'dev', split_axis=0, concat_axis=0, tiled=True)]
where the time goes in v7:
time: 96.9 us; the launch traced here: 96.4 us
  Pallas kernels  59.1 us (61%)
  starting transfers between devices  19.9 us (21%)
  waiting for transfers between devices  14 us (14%)
  local copies, waits for them, and re-layouts  2.63 us (3%)
    pallas_call x2, Pallas kernels, pair_products(): pl.pallas_call(functools.partial(pair_kernel, first, steps, len(replies))...  48.2 us
    all_to_all x2, waiting for transfers between devices, shards(): got = lax.all_to_all(found, 'dev', split_axis=0, concat_axis=0, tiled=True)  14 us
    all_to_all x2, starting transfers between devices, shards(): got = lax.all_to_all(found, 'dev', split_axis=0, concat_axis=0, tiled=True)  11.4 us
    all_to_all x1, starting transfers between devices, shards(): lax.all_to_all(wanted, 'dev', split_axis=0, concat_axis=0, tiled=True)  8.59 us
    pallas_call x1, Pallas kernels, pick(): pl.pallas_call(pick_kernel, out_shape=jax.ShapeDtypeStruct((CL_DEV, 32, 1...  5.07 us
    pallas_call x2, Pallas kernels, reply(): pl.pallas_call(functools.partial(reply_kernel, phase), in_specs=[pl.Block...  3.47 us
    unnamed x8, local copies, waits for them, and re-layouts  2.63 us
    pallas_call x1, Pallas kernels, plan(): pl.pallas_call(plan_kernel, out_shape=[jax.ShapeDtypeStruct((members, 128...  2.33 us
  transfers between devices with their start and end apart: 3, of which 1 were waited for; matrix products, arithmetic and copies ran while one was open for 0% of the time, Pallas kernels for 32%

profile of v7, /device:TPU:1, one launch (start us, length us, event | category | flops | bytes accessed | tf_op | source)
XLA Modules:
  0.0 96.4 jit_solution(1650155977292960231)
XLA Ops:
  0.6 2.3 %plan.1 = (s32[32,128]{1,0:T(8,128)}, s32[8,32]{1,0:T(8,128)}) custom-call(s32[1,32]{1,0:T(1,128)} %bitcast.14, s32[1,32]{1,0:T(1,128)} %bitcast.15, s32[2,32]{1,0:T(2,128)} %bitcast.13, s32[1,32]{1,0:T(1,128)} %bitcast.16), custom_call_target="tpu_custom_call" | custom-call | tf_op jit(solution)/shard_map/plan/pallas_call | solution.py:151
  3.0 8.6 %all-to-all-start = ((s32[32,1,128]{2,1,0:T(1,128)}), s32[32,1,128]{2,1,0:T(1,128)S(1)}, u32[]{:S(2)}, u32[]{:S(2)}) async-start(s32[32,1,128]{2,1,0:T(1,128)} %bitcast.12), calls=%async_computation | async-start | bytes 32768 | tf_op jit(solution)/shard_map/all_to_all | solution.py:373
  11.6 0.0 copy-start
  11.6 0.9 copy-done
  12.5 0.0 copy-start.1
  12.5 0.8 copy-done.1
  13.4 0.0 copy-start.2
  13.4 0.8 copy-done.2
  14.2 0.0 copy-start.3
  14.2 5.1 %pick.1.points_ref = f32[16,32,128]{2,1,0:T(8,128)S(1)} custom-call(s32[1,16384]{1,0:T(1,128)S(1)} %copy-done.1, f32[3,16384]{1,0:T(4,128)S(1)} %copy-done, f32[128,128]{1,0:T(8,128)S(1)} %bitcast.11), custom_call_target="tpu_custom_call" | custom-call | flops 5000000000 | bytes 600000 | tf_op jit(solution)/shard_map/pick/pallas_call | solution.py:69
  19.3 0.0 all-to-all-done
  19.3 1.7 %reply.2 = f32[32,56,128]{2,1,0:T(8,128)} custom-call(s32[32,128]{1,0:T(8,128)S(1)} %bitcast.9, f32[16,32,128]{2,1,0:T(8,128)S(1)} %pick.1.points_ref), custom_call_target="tpu_custom_call" | custom-call | bytes 4000000 | tf_op jit(solution)/shard_map/reply/pallas_call | solution.py:178
  21.0 7.4 %all-to-all-start.1 = ((f32[32,56,128]{2,1,0:T(8,128)}), f32[32,56,128]{2,1,0:T(8,128)S(1)}, u32[]{:S(2)}, u32[]{:S(2)}) async-start(f32[32,56,128]{2,1,0:T(8,128)} %reply.2), calls=%async_computation.1 | async-start | bytes 1835008 | tf_op jit(solution)/shard_map/all_to_all | solution.py:378
  28.4 1.8 %reply.3 = f32[32,56,128]{2,1,0:T(8,128)} custom-call(s32[32,128]{1,0:T(8,128)S(1)} %bitcast.10, f32[16,32,128]{2,1,0:T(8,128)S(1)} %pick.1.points_ref), custom_call_target="tpu_custom_call" | custom-call | bytes 4000000 | tf_op jit(solution)/shard_map/reply/pallas_call | solution.py:178
  30.2 14.0 %all-to-all-done.1.refs_0_ = f32[32,56,128]{2,1,0:T(8,128)S(1)} async-done(((f32[32,56,128]{2,1,0:T(8,128)}), f32[32,56,128]{2,1,0:T(8,128)S(1)}, u32[]{:S(2)}, u32[]{:S(2)}) %all-to-all-start.1) | async-done | bytes 917536 | tf_op jit(solution)/shard_map/all_to_all | solution.py:378
  44.2 4.0 %all-to-all-start.2 = ((f32[32,56,128]{2,1,0:T(8,128)}), f32[32,56,128]{2,1,0:T(8,128)S(1)}, u32[]{:S(2)}, u32[]{:S(2)}) async-start(f32[32,56,128]{2,1,0:T(8,128)} %reply.3), calls=%async_computation.2 | async-start | bytes 1835008 | tf_op jit(solution)/shard_map/all_to_all | solution.py:378
  48.1 0.0 copy-done.3
  48.1 24.1 %pairs.2 = (bf16[32,1024,128]{2,1,0:T(8,128)(2,1)}, bf16[32,128,1024]{2,1,0:T(8,128)(2,1)}) custom-call(s32[8,32]{1,0:T(8,128)S(1)} %copy-done.3, f32[32,56,128]{2,1,0:T(8,128)S(1)} %all-to-all-done.1.refs_0_, bf16[32,1024,128]{2,1,0:T(8,128)(2,1)} %refs_3_.1, bf16[32,1024,128]{2,1,0:T(8,128)(2,1)} %refs_3_.1), custom_call_target="tpu_custom_call" | custom-call | flops 25769803776 | bytes 12800000 | tf_op jit(solution)/shard_map/pairs/pallas_call | solution.py:328
  72.3 0.0 all-to-all-done.2.refs_1_
  72.3 24.1 %pairs.3 = (bf16[32,1024,128]{2,1,0:T(8,128)(2,1)}, bf16[32,128,1024]{2,1,0:T(8,128)(2,1)}) custom-call(s32[8,32]{1,0:T(8,128)S(1)} %copy-done.3, f32[32,56,128]{2,1,0:T(8,128)S(1)} %all-to-all-done.1.refs_0_, f32[32,56,128]{2,1,0:T(8,128)S(1)} %all-to-all-done.2.refs_1_, ...), custom_call_target="tpu_custom_call", output_to_operand_aliasing={{0}: (5, {}), {1}: (6, {})} | custom-call | flops 25769803776 | bytes 12800000 | tf_op jit(solution)/shard_map/pairs/pallas_call | solution.py:328
Async XLA Ops:
  3.0 16.3 %all-to-all-start = ((s32[32,1,128]{2,1,0:T(1,128)}), s32[32,1,128]{2,1,0:T(1,128)S(1)}, u32[]{:S(2)}, u32[]{:S(2)}) async-start(s32[32,1,128]{2,1,0:T(1,128)} %bitcast.12), calls=%async_computation | async-start | bytes 32768 | tf_op jit(solution)/shard_map/all_to_all | solution.py:373
  11.6 1.0 copy-start
  12.5 0.8 copy-start.1
  13.4 0.8 copy-start.2
  14.2 33.9 %copy-start.3 = (s32[8,32]{1,0:T(8,128)S(1)}, s32[8,32]{1,0:T(8,128)}, u32[]{:S(2)}) copy-start(s32[8,32]{1,0:T(8,128)} %get-tuple-element.6.places) | copy-start | bytes 3076
  21.0 23.2 %all-to-all-start.1 = ((f32[32,56,128]{2,1,0:T(8,128)}), f32[32,56,128]{2,1,0:T(8,128)S(1)}, u32[]{:S(2)}, u32[]{:S(2)}) async-start(f32[32,56,128]{2,1,0:T(8,128)} %reply.2), calls=%async_computation.1 | async-start | bytes 1835008 | tf_op jit(solution)/shard_map/all_to_all | solution.py:378
  44.2 28.1 %all-to-all-start.2 = ((f32[32,56,128]{2,1,0:T(8,128)}), f32[32,56,128]{2,1,0:T(8,128)S(1)}, u32[]{:S(2)}, u32[]{:S(2)}) async-start(f32[32,56,128]{2,1,0:T(8,128)} %reply.3), calls=%async_computation.2 | async-start | bytes 1835008 | tf_op jit(solution)/shard_map/all_to_all | solution.py:378

commit v8 on v7

--- a/solution.py
+++ b/solution.py
@@ -22,7 +22,7 @@
 def contract(a, b, dim_a, dim_b):
     return lax.dot_general(a, b, (((dim_a,), (dim_b,)), ((), ())), preferred_element_type=f32)
 
-PICK_TURN = 8
+PICK_TURN = 16
 LANES = 256
 
 

time: 96.9 us -> 96.9 us (level)
  no operation moved by 1% of the time
where the time goes in v8:
time: 96.9 us; the launch traced here: 96.3 us
  Pallas kernels  58.8 us (61%)
  starting transfers between devices  20 us (21%)
  waiting for transfers between devices  14 us (14%)
  local copies, waits for them, and re-layouts  2.63 us (3%)
    pallas_call x2, Pallas kernels, pair_products(): pl.pallas_call(functools.partial(pair_kernel, first, steps, len(replies))...  48.2 us
    all_to_all x2, waiting for transfers between devices, shards(): got = lax.all_to_all(found, 'dev', split_axis=0, concat_axis=0, tiled=True)  14 us
    all_to_all x2, starting transfers between devices, shards(): got = lax.all_to_all(found, 'dev', split_axis=0, concat_axis=0, tiled=True)  11.4 us
    all_to_all x1, starting transfers between devices, shards(): lax.all_to_all(wanted, 'dev', split_axis=0, concat_axis=0, tiled=True)  8.59 us
    pallas_call x1, Pallas kernels, pick(): pl.pallas_call(pick_kernel, out_shape=jax.ShapeDtypeStruct((CL_DEV, 32, 1...  4.81 us
    pallas_call x2, Pallas kernels, reply(): pl.pallas_call(functools.partial(reply_kernel, phase), in_specs=[pl.Block...  3.47 us
    unnamed x8, local copies, waits for them, and re-layouts  2.63 us
    pallas_call x1, Pallas kernels, plan(): pl.pallas_call(plan_kernel, out_shape=[jax.ShapeDtypeStruct((members, 128...  2.33 us
  transfers between devices with their start and end apart: 3, of which 1 were waited for; matrix products, arithmetic and copies ran while one was open for 0% of the time, Pallas kernels for 32%

profile of v8, /device:TPU:1, one launch (start us, length us, event | category | flops | bytes accessed | tf_op | source)
XLA Modules:
  0.0 96.3 jit_solution(6787351333586344794)
XLA Ops:
  0.6 2.3 %plan.1 = (s32[32,128]{1,0:T(8,128)}, s32[8,32]{1,0:T(8,128)}) custom-call(s32[1,32]{1,0:T(1,128)} %bitcast.14, s32[1,32]{1,0:T(1,128)} %bitcast.15, s32[2,32]{1,0:T(2,128)} %bitcast.13, s32[1,32]{1,0:T(1,128)} %bitcast.16), custom_call_target="tpu_custom_call" | custom-call | tf_op jit(solution)/shard_map/plan/pallas_call | solution.py:151
  3.0 8.6 %all-to-all-start = ((s32[32,1,128]{2,1,0:T(1,128)}), s32[32,1,128]{2,1,0:T(1,128)S(1)}, u32[]{:S(2)}, u32[]{:S(2)}) async-start(s32[32,1,128]{2,1,0:T(1,128)} %bitcast.12), calls=%async_computation | async-start | bytes 32768 | tf_op jit(solution)/shard_map/all_to_all | solution.py:373
  11.6 0.0 copy-start
  11.6 0.9 copy-done
  12.5 0.0 copy-start.1
  12.5 0.8 copy-done.1
  13.4 0.0 copy-start.2
  13.4 0.8 copy-done.2
  14.2 0.0 copy-start.3
  14.2 4.8 %pick.1.points_ref = f32[16,32,128]{2,1,0:T(8,128)S(1)} custom-call(s32[1,16384]{1,0:T(1,128)S(1)} %copy-done.1, f32[3,16384]{1,0:T(4,128)S(1)} %copy-done, f32[128,128]{1,0:T(8,128)S(1)} %bitcast.11), custom_call_target="tpu_custom_call" | custom-call | flops 5000000000 | bytes 600000 | tf_op jit(solution)/shard_map/pick/pallas_call | solution.py:69
  19.0 0.0 all-to-all-done
  19.0 1.7 %reply.2 = f32[32,56,128]{2,1,0:T(8,128)} custom-call(s32[32,128]{1,0:T(8,128)S(1)} %bitcast.9, f32[16,32,128]{2,1,0:T(8,128)S(1)} %pick.1.points_ref), custom_call_target="tpu_custom_call" | custom-call | bytes 4000000 | tf_op jit(solution)/shard_map/reply/pallas_call | solution.py:178
  20.7 7.4 %all-to-all-start.1 = ((f32[32,56,128]{2,1,0:T(8,128)}), f32[32,56,128]{2,1,0:T(8,128)S(1)}, u32[]{:S(2)}, u32[]{:S(2)}) async-start(f32[32,56,128]{2,1,0:T(8,128)} %reply.2), calls=%async_computation.1 | async-start | bytes 1835008 | tf_op jit(solution)/shard_map/all_to_all | solution.py:378
  28.1 1.8 %reply.3 = f32[32,56,128]{2,1,0:T(8,128)} custom-call(s32[32,128]{1,0:T(8,128)S(1)} %bitcast.10, f32[16,32,128]{2,1,0:T(8,128)S(1)} %pick.1.points_ref), custom_call_target="tpu_custom_call" | custom-call | bytes 4000000 | tf_op jit(solution)/shard_map/reply/pallas_call | solution.py:178
  29.9 14.0 %all-to-all-done.1.refs_0_ = f32[32,56,128]{2,1,0:T(8,128)S(1)} async-done(((f32[32,56,128]{2,1,0:T(8,128)}), f32[32,56,128]{2,1,0:T(8,128)S(1)}, u32[]{:S(2)}, u32[]{:S(2)}) %all-to-all-start.1) | async-done | bytes 917536 | tf_op jit(solution)/shard_map/all_to_all | solution.py:378
  43.9 4.0 %all-to-all-start.2 = ((f32[32,56,128]{2,1,0:T(8,128)}), f32[32,56,128]{2,1,0:T(8,128)S(1)}, u32[]{:S(2)}, u32[]{:S(2)}) async-start(f32[32,56,128]{2,1,0:T(8,128)} %reply.3), calls=%async_computation.2 | async-start | bytes 1835008 | tf_op jit(solution)/shard_map/all_to_all | solution.py:378
  47.9 0.0 copy-done.3
  47.9 24.1 %pairs.2 = (bf16[32,1024,128]{2,1,0:T(8,128)(2,1)}, bf16[32,128,1024]{2,1,0:T(8,128)(2,1)}) custom-call(s32[8,32]{1,0:T(8,128)S(1)} %copy-done.3, f32[32,56,128]{2,1,0:T(8,128)S(1)} %all-to-all-done.1.refs_0_, bf16[32,1024,128]{2,1,0:T(8,128)(2,1)} %refs_3_.1, bf16[32,1024,128]{2,1,0:T(8,128)(2,1)} %refs_3_.1), custom_call_target="tpu_custom_call" | custom-call | flops 25769803776 | bytes 12800000 | tf_op jit(solution)/shard_map/pairs/pallas_call | solution.py:328
  72.0 0.0 all-to-all-done.2.refs_1_
  72.0 24.1 %pairs.3 = (bf16[32,1024,128]{2,1,0:T(8,128)(2,1)}, bf16[32,128,1024]{2,1,0:T(8,128)(2,1)}) custom-call(s32[8,32]{1,0:T(8,128)S(1)} %copy-done.3, f32[32,56,128]{2,1,0:T(8,128)S(1)} %all-to-all-done.1.refs_0_, f32[32,56,128]{2,1,0:T(8,128)S(1)} %all-to-all-done.2.refs_1_, ...), custom_call_target="tpu_custom_call", output_to_operand_aliasing={{0}: (5, {}), {1}: (6, {})} | custom-call | flops 25769803776 | bytes 12800000 | tf_op jit(solution)/shard_map/pairs/pallas_call | solution.py:328
Async XLA Ops:
  3.0 16.1 %all-to-all-start = ((s32[32,1,128]{2,1,0:T(1,128)}), s32[32,1,128]{2,1,0:T(1,128)S(1)}, u32[]{:S(2)}, u32[]{:S(2)}) async-start(s32[32,1,128]{2,1,0:T(1,128)} %bitcast.12), calls=%async_computation | async-start | bytes 32768 | tf_op jit(solution)/shard_map/all_to_all | solution.py:373
  11.6 1.0 copy-start
  12.5 0.8 copy-start.1
  13.4 0.8 copy-start.2
  14.2 33.7 %copy-start.3 = (s32[8,32]{1,0:T(8,128)S(1)}, s32[8,32]{1,0:T(8,128)}, u32[]{:S(2)}) copy-start(s32[8,32]{1,0:T(8,128)} %get-tuple-element.6.places) | copy-start | bytes 3076
  20.7 23.2 %all-to-all-start.1 = ((f32[32,56,128]{2,1,0:T(8,128)}), f32[32,56,128]{2,1,0:T(8,128)S(1)}, u32[]{:S(2)}, u32[]{:S(2)}) async-start(f32[32,56,128]{2,1,0:T(8,128)} %reply.2), calls=%async_computation.1 | async-start | bytes 1835008 | tf_op jit(solution)/shard_map/all_to_all | solution.py:378
  43.9 28.1 %all-to-all-start.2 = ((f32[32,56,128]{2,1,0:T(8,128)}), f32[32,56,128]{2,1,0:T(8,128)S(1)}, u32[]{:S(2)}, u32[]{:S(2)}) async-start(f32[32,56,128]{2,1,0:T(8,128)} %reply.3), calls=%async_computation.2 | async-start | bytes 1835008 | tf_op jit(solution)/shard_map/all_to_all | solution.py:378
